TPU v7x, 256 devices: a whole 4x4x8 slice. The times are simulated.
256 devices in a mesh: batch: 8 (over x, core), seq: 32 (over y, z).
Axes of the slice: x: 4, y: 4, z: 8, core: 2. Of those that a mesh axis runs over, the one named last changes fastest.
Arguments:
- queries: bfloat16 [98304, 2048], P(('batch', 'seq')), parts along dimension 0, may hold values from -6 to 6
- cotangent: bfloat16 [98304, 2048], P(('batch', 'seq')), parts along dimension 0, may hold values from -6 to 6
- pool: bfloat16 [512, 128, 448], P(('batch', 'seq')), parts along dimension 0, may hold values from -6 to 6
- key_weight: bfloat16 [448, 2048], P('seq'), may hold values from -0.25 to 0.25
- value_weight: bfloat16 [448, 2048], P('seq'), may hold values from -0.25 to 0.25
- score_bias: float32 [16, 64, 256], replicated, may hold values from -300 to 300
- neighbours: int32 [1536, 2], P(('batch', 'seq')), parts along dimension 0, may hold values from 0 to 63, as said below
- place: int32 [512], P('batch'), parts along dimension 0, may hold values from 0 to 63, as said below
Outputs:
- attended: bfloat16 [98304, 2048], P(('batch', 'seq')), parts along dimension 0
- query_grad: bfloat16 [98304, 2048], P(('batch', 'seq')), parts along dimension 0
- pool_grad: float32 [512, 128, 448], P(('batch', 'seq')), parts along dimension 0
There are 8 independent parts, one for each index of `batch`. A program takes and returns all parts, laid end to end along the dimension named above; an argument that names none is the same for every part. Nothing has to cross between parts.
Inputs may be any that keep to these rules, and one draw needn't show every extreme that they name: `neighbours`: the two blocks of a span differ. The owner of block b is place[b] // 2; among the 12 reads of one device's spans at most 1 fall on blocks of one owner, and on every device some owner gets exactly 1. `place`: A permutation of the block numbers.
All inputs are finite; a program needn't handle non-finite values.
Results may differ from a plain program's by a relative error of at most 0.015.
Values may be sent and summed in bfloat16 or wider, within the bound.
A program may use at most 128 MiB of HBM per device.

v0:
```python
import math

import jax
import jax.numpy as jnp
from jax import lax
from jax.sharding import PartitionSpec as P

HEADS = 16
HDIM = 128
E = 448
SPAN = 64
NB = 128


def on_device(queries, cotangent, pool, key_weight, value_weight, score_bias, neighbours, place):
    score_scale = 1.0 / math.sqrt(HDIM)
    peer_count = lax.axis_size("seq")
    spans = queries.shape[0] // SPAN
    read_count = 2 * spans
    owned_count = pool.shape[0]
    head_width = HEADS * HDIM
    capacity = (read_count + peer_count - 1) // peer_count
    slot_count = peer_count * capacity
    position = place[neighbours].reshape(read_count)
    holder = position // owned_count
    local_row = position % owned_count
    read_order = jnp.arange(read_count)
    earlier = (holder[:, None] == holder[None, :]) & (read_order[:, None] > read_order[None, :])
    target = holder * capacity + jnp.sum(earlier, axis=1)
    marked = target[None, :] == jnp.arange(slot_count)[:, None]
    wanted = jnp.max(jnp.where(marked, local_row[None, :], -1), axis=1).reshape(
        peer_count, capacity
    )
    asked_rows = lax.all_to_all(wanted, "seq", split_axis=0, concat_axis=0, tiled=True)
    chooser = (asked_rows[:, :, None] == jnp.arange(owned_count)[None, None, :]).astype(
        jnp.bfloat16
    )
    outgoing = jnp.einsum(
        "scp,pte->scte", chooser, pool, preferred_element_type=jnp.float32
    ).astype(jnp.bfloat16)
    arrived = lax.all_to_all(outgoing, "seq", split_axis=0, concat_axis=0, tiled=True)
    encoded = arrived.reshape(slot_count, NB, E)[target]
    flat_enc = encoded.reshape(read_count * NB, E)
    full_key, full_value = (
        lax.all_gather(key_weight, "seq", axis=0, tiled=True),
        lax.all_gather(value_weight, "seq", axis=0, tiled=True),
    )
    key_rows = jnp.dot(flat_enc, full_key, preferred_element_type=jnp.float32).astype(jnp.bfloat16)
    value_rows = jnp.dot(flat_enc, full_value, preferred_element_type=jnp.float32).astype(
        jnp.bfloat16
    )
    query_heads = queries.reshape(spans, SPAN, HEADS, HDIM)
    grad_heads = cotangent.reshape(spans, SPAN, HEADS, HDIM)
    key_heads = key_rows.reshape(spans, 2 * NB, HEADS, HDIM)
    value_heads = value_rows.reshape(spans, 2 * NB, HEADS, HDIM)
    scores = (
        jnp.einsum("cihd,cthd->chit", query_heads, key_heads, preferred_element_type=jnp.float32)
        * score_scale
        + score_bias[None]
    )
    row_top = jnp.max(scores, axis=-1, keepdims=True)
    raw_exp = jnp.exp(scores - row_top)
    attn_probs = raw_exp / jnp.sum(raw_exp, axis=-1, keepdims=True)
    probs_low = attn_probs.astype(jnp.bfloat16)
    attended = jnp.einsum(
        "chit,cthd->cihd", probs_low, value_heads, preferred_element_type=jnp.float32
    ).astype(jnp.bfloat16)
    row_delta = jnp.sum(grad_heads.astype(jnp.float32) * attended.astype(jnp.float32), axis=-1)
    prob_grad = jnp.einsum(
        "cihd,cthd->chit", grad_heads, value_heads, preferred_element_type=jnp.float32
    )
    score_grad = attn_probs * (prob_grad - jnp.transpose(row_delta, (0, 2, 1))[..., None])
    dscore_low = score_grad.astype(jnp.bfloat16)
    query_grad = (
        jnp.einsum("chit,cthd->cihd", dscore_low, key_heads, preferred_element_type=jnp.float32)
        * score_scale
    ).astype(jnp.bfloat16)
    key_grad = (
        jnp.einsum("chit,cihd->cthd", dscore_low, query_heads, preferred_element_type=jnp.float32)
        * score_scale
    ).astype(jnp.bfloat16)
    value_grad = jnp.einsum(
        "chit,cihd->cthd", probs_low, grad_heads, preferred_element_type=jnp.float32
    ).astype(jnp.bfloat16)
    key_grad = key_grad.reshape(read_count * NB, head_width)
    value_grad = value_grad.reshape(read_count * NB, head_width)
    read_grad = jnp.dot(key_grad, full_key.T, preferred_element_type=jnp.float32)
    read_grad = read_grad + jnp.dot(value_grad, full_value.T, preferred_element_type=jnp.float32)
    read_grad = read_grad.astype(jnp.bfloat16).reshape(read_count, NB, E)
    outgoing_grads = jnp.zeros((slot_count, NB, E), jnp.bfloat16).at[target].set(read_grad)
    returned = lax.all_to_all(
        outgoing_grads.reshape(peer_count, capacity, NB, E),
        "seq",
        split_axis=0,
        concat_axis=0,
        tiled=True,
    )
    pool_grad = jnp.einsum("scp,scte->pte", chooser, returned, preferred_element_type=jnp.float32)
    return (
        attended.reshape(spans * SPAN, head_width),
        query_grad.reshape(spans * SPAN, head_width),
        pool_grad,
    )


def solution(mesh):
    in_specs = (
        P(("batch", "seq"), None),
        P(("batch", "seq"), None),
        P(("batch", "seq"), None, None),
        P("seq", None),
        P("seq", None),
        P(),
        P(("batch", "seq"), None),
        P("batch"),
    )
    out_specs = (
        P(("batch", "seq"), None),
        P(("batch", "seq"), None),
        P(("batch", "seq"), None, None),
    )
    return jax.shard_map(
        on_device, mesh=mesh, in_specs=in_specs, out_specs=out_specs, check_vma=False
    )
```

profile of v0, /device:TPU:4, one launch (start us, length us, event | category | flops | bytes accessed | tf_op | source)
XLA Modules:
  0.0 391.8 jit_solution(5336866779387316455)
XLA Ops:
  10.4 11.5 %all-to-all-start = ((s32[32,1,1]{2,1,0:T(1,128)}), s32[32,1,1]{2,1,0:T(1,128)S(1)}, u32[]{:S(2)}, u32[]{:S(2)}) async-start(s32[32,1,1]{2,1,0:T(1,128)} %copy.90), calls=%async_computation | async-start | bytes 32768 | tf_op jit(solution)/shard_map/all_to_all | solution.py:34
  22.6 9.0 %all-to-all-done = s32[32,1,1]{2,1,0:T(1,128)S(1)} async-done(((s32[32,1,1]{2,1,0:T(1,128)}), s32[32,1,1]{2,1,0:T(1,128)S(1)}, u32[]{:S(2)}, u32[]{:S(2)}) %all-to-all-start) | async-done | bytes 160 | tf_op jit(solution)/shard_map/all_to_all | solution.py:34
  33.5 3.4 copy.92
  36.8 5.0 %all-to-all-start.1 = ((bf16[32,1,128,448]{2,3,1,0:T(8,128)(2,1)}), bf16[32,1,128,448]{2,3,1,0:T(8,128)(2,1)}, u32[]{:S(2)}, u32[]{:S(2)}) async-start(bf16[32,1,128,448]{2,3,1,0:T(8,128)(2,1)} %copy.92), calls=%async_computation.1 | async-start | bytes 7340032 | tf_op jit(solution)/shard_map/all_to_all | solution.py:41
  42.6 1.6 copy.116
  44.6 84.8 %all-gather.5.cloned.1.call-done = bf16[32,14,2048]{2,1,0:T(8,128)(2,1)} async-done(((bf16[1,14,2048]{2,1,0:T(8,128)(2,1)}), bf16[32,14,2048]{2,1,0:T(8,128)(2,1)}) %all-gather.5.cloned.1.call-update) | async-done | bytes 1835024 | tf_op jit(solution)/shard_map/all_gather | solution.py:46
  129.4 4.2 %reshape.317 = bf16[448,2048]{1,0:T(8,128)(2,1)} reshape(bf16[32,14,2048]{2,1,0:T(8,128)(2,1)} %all-gather.5.cloned.1.call-done) | data formatting | bytes 3670016
  133.6 76.4 %all-gather.7.cloned.1.call-done = bf16[32,14,2048]{2,1,0:T(8,128)(2,1)} async-done(((bf16[1,14,2048]{2,1,0:T(8,128)(2,1)}), bf16[32,14,2048]{2,1,0:T(8,128)(2,1)}) %all-gather.7.cloned.1.call-update) | async-done | bytes 1835024 | tf_op jit(solution)/shard_map/all_gather | solution.py:45
  210.0 3.7 reshape.319
  213.8 2.8 gather_fusion.1
  216.6 1.6 copy.93
  218.2 5.4 %fusion.29 = bf16[192,8,16,128]{3,1,2,0:T(8,128)(2,1)S(1)} fusion(bf16[1536,448]{1,0:T(8,128)(2,1)} %bitcast.127, bf16[448,2048]{1,0:T(8,128)(2,1)} %reshape.317), kind=kOutput, calls=%fused_computation.39 | convolution fusion | flops 2821718016 | bytes 9502720 | tf_op jit(solution)/shard_map/dot_general | solution.py:49
  223.6 5.0 %copy.114 = bf16[192,8,16,128]{3,2,1,0:T(8,128)(2,1)} copy(bf16[192,8,16,128]{3,1,2,0:T(8,128)(2,1)S(1)} %fusion.29) | data formatting | bytes 12582912
  228.6 3.6 fusion.30
  232.2 2.3 copy.112
  234.6 2.3 fusion.15
  237.2 4.4 %fusion.63 = (f32[6,16,64]{2,1,0:T(8,128)S(1)}, f32[6,16,64,256]{3,2,1,0:T(8,128)}) fusion(f32[6,16,256,64]{2,3,1,0:T(8,128)S(1)} %fusion.15, f32[16,64,256]{2,1,0:T(8,128)S(1)} %copy-done.13), kind=kOutput, calls=%fused_computation.82 | output fusion | flops 9437439 | bytes 13656064 | tf_op jit(solution)/shard_map/sub | solution.py:62
  241.6 6.9 %convert_bitcast_fusion = bf16[6,256,16,128]{3,1,2,0:T(8,128)(2,1)} fusion(bf16[6,64,16,128]{3,2,1,0:T(8,128)(2,1)S(1)} %bitcast.124, f32[6,16,64,256]{3,2,1,0:T(8,128)} %get-tuple-element.21, f32[6,16,64]{2,1,0:T(8,128)S(1)} %get-tuple-element.20), kind=kOutput, calls=%fused_computation.17 | convolution fusion | flops 408944640 | bytes 14180352 | tf_op jit(solution)/shard_map/chit,cihd->cthd/dot_general | solution.py:82
  248.6 5.8 %multiply_reduce_fusion = (f32[6,64,16]{1,2,0:T(8,128)S(1)}, bf16[6,64,16,128]{3,1,2,0:T(8,128)(2,1)}) fusion(bf16[6,64,16,128]{3,2,1,0:T(8,128)(2,1)S(1)} %bitcast.125, bf16[6,256,16,128]{3,2,1,0:T(8,128)(2,1)S(1)} %bitcast.113, f32[6,16,64,256]{3,2,1,0:T(8,128)} %get-tuple-element.21, f32[6,16,64]{2,1,0:T(8,128)S(1)} %get-tuple-element.20), kind=kOutput, calls=%fused_computation.33 | convolution fusion | flops 409724928 | bytes 15777792 | tf_op jit(solution)/shard_map/chit,cthd->cihd/dot_general | solution.py:65
  254.4 8.1 %fusion.8 = bf16[6,16,64,256]{3,2,1,0:T(8,128)(2,1)} fusion(f32[6,16,64]{2,1,0:T(8,128)S(1)} %bitcast.132, f32[6,16,64,256]{3,2,1,0:T(8,128)} %get-tuple-element.21, f32[6,16,64]{2,1,0:T(8,128)S(1)} %get-tuple-element.20, bf16[6,256,16,128]{3,2,1,0:T(8,128)(2,1)S(1)} %bitcast.114, bf16[6,64,16,128]{3,2,1,0:T(8,128)(2,1)S(1)} %bitcast.126), kind=kOutput, calls=%fused_computation.15 | convolution fusion | flops 408944640 | bytes 17350656 | tf_op jit(solution)/shard_map/cihd,cthd->chit/dot_general | solution.py:69
  262.4 4.1 %copy.106 = bf16[6,256,16,128]{3,2,1,0:T(8,128)(2,1)S(1)} copy(bf16[6,256,16,128]{3,1,2,0:T(8,128)(2,1)S(1)} %bitcast.116) | data formatting | bytes 12582912 | tf_op jit(solution)/shard_map/convert_element_type | solution.py:84
  266.5 4.7 %fusion.2 = f32[1536,448]{0,1:T(8,128)} fusion(bf16[448,2048]{1,0:T(8,128)(2,1)S(1)} %copy-done.7, bf16[192,8,16,128]{3,2,1,0:T(8,128)(2,1)S(1)} %bitcast.118), kind=kOutput, calls=%fused_computation.8 | convolution fusion | flops 2818572288 | bytes 10878976 | tf_op jit(solution)/shard_map/dot_general | solution.py:88
  271.2 2.7 fusion.1
  273.9 4.1 %copy.104 = bf16[6,256,16,128]{3,2,1,0:T(8,128)(2,1)S(1)} copy(bf16[6,256,16,128]{3,1,2,0:T(8,128)(2,1)S(1)} %fusion.1) | data formatting | bytes 12582912 | tf_op jit(solution)/shard_map/convert_element_type | solution.py:81
  278.0 4.8 %fusion.26 = bf16[1536,448]{0,1:T(8,128)(2,1)S(1)} fusion(f32[1536,448]{0,1:T(8,128)} %fusion.2, bf16[448,2048]{1,0:T(8,128)(2,1)S(1)} %copy-done.6, bf16[192,8,16,128]{3,2,1,0:T(8,128)(2,1)S(1)} %bitcast.117), kind=kOutput, calls=%fused_computation.38 | convolution fusion | flops 2819948544 | bytes 12255232 | tf_op jit(solution)/shard_map/dot_general | solution.py:87
  284.4 2.7 broadcast_in_dim.19
  287.1 5.0 %scatter_fusion = bf16[32,128,448]{1,2,0:T(8,128)(2,1)} fusion(bf16[32,128,448]{1,2,0:T(8,128)(2,1)} %broadcast_in_dim.19, s32[12]{0:T(128)S(1)} %fusion.57, bf16[12,128,448]{1,2,0:T(8,128)(2,1)S(1)} %copy.108), kind=kCustom, calls=%fused_computation.2 | custom fusion | bytes 4128816 | tf_op jit(solution)/shard_map/scatter | solution.py:90
  292.1 6.4 %all-to-all-start.2 = ((bf16[32,1,128,448]{2,3,1,0:T(8,128)(2,1)}), bf16[32,1,128,448]{2,3,1,0:T(8,128)(2,1)}, u32[]{:S(2)}, u32[]{:S(2)}) async-start(bf16[32,1,128,448]{2,3,1,0:T(8,128)(2,1)} %bitcast.108), calls=%async_computation.2 | async-start | bytes 7340032 | tf_op jit(solution)/shard_map/all_to_all | solution.py:91
  298.5 4.8 %fusion.42 = bf16[6,64,16,128]{3,1,2,0:T(8,128)(2,1)S(1)} fusion(bf16[6,16,64,256]{3,2,1,0:T(8,128)(2,1)S(1)} %copy-done.4, bf16[6,256,16,128]{3,2,1,0:T(8,128)(2,1)} %bitcast.107), kind=kOutput, calls=%fused_computation.46 | convolution fusion | flops 404226048 | bytes 11010048 | tf_op jit(solution)/shard_map/chit,cthd->cihd/dot_general | solution.py:75
  305.7 2.7 copy_bitcast_fusion
  308.4 71.3 %all-to-all-done.2 = bf16[32,1,128,448]{2,3,1,0:T(8,128)(2,1)} async-done(((bf16[32,1,128,448]{2,3,1,0:T(8,128)(2,1)}), bf16[32,1,128,448]{2,3,1,0:T(8,128)(2,1)}, u32[]{:S(2)}, u32[]{:S(2)}) %all-to-all-start.2) | async-done | bytes 3670048 | tf_op jit(solution)/shard_map/all_to_all | solution.py:91
  379.7 4.2 %fusion.18 = f32[2,128,448]{1,0,2:T(2,128)S(1)} fusion(bf16[32,1,128,448]{2,3,1,0:T(8,128)(2,1)} %all-to-all-done.2, s32[32]{0:T(128)S(1)} %reduce), kind=kOutput, calls=%fused_computation.28 | convolution fusion | flops 7340096 | bytes 4128896 | tf_op jit(solution)/shard_map/scp,scte->pte/dot_general | solution.py:98
  (63 shorter events, 12.1 us)
Async XLA Ops:
  7.2 25.1 %copy-start = (bf16[2,128,448]{1,2,0:T(8,128)(2,1)S(1)}, bf16[2,128,448]{1,2,0:T(8,128)(2,1)}, u32[]{:S(2)}) copy-start(bf16[2,128,448]{1,2,0:T(8,128)(2,1)} %param.10) | copy-start | bytes 688132
  10.4 21.2 %all-to-all-start = ((s32[32,1,1]{2,1,0:T(1,128)}), s32[32,1,1]{2,1,0:T(1,128)S(1)}, u32[]{:S(2)}, u32[]{:S(2)}) async-start(s32[32,1,1]{2,1,0:T(1,128)} %copy.90), calls=%async_computation | async-start | bytes 32768 | tf_op jit(solution)/shard_map/all_to_all | solution.py:34
  21.9 107.5 %all-gather.5.cloned.1.call-start = ((), (), s32[]{:S(2)}) async-start(), calls=%async_computation.3 | async-start | bytes 2162688 | tf_op jit(solution)/shard_map/all_gather | solution.py:46
  36.8 5.8 %copy-start.8 = (bf16[384,2048]{1,0:T(8,128)(2,1)S(1)}, bf16[384,2048]{1,0:T(8,128)(2,1)}, u32[]{:S(2)}) copy-start(bf16[384,2048]{1,0:T(8,128)(2,1)} %param.9) | copy-start | bytes 4718596
  36.8 176.9 %all-to-all-start.1 = ((bf16[32,1,128,448]{2,3,1,0:T(8,128)(2,1)}), bf16[32,1,128,448]{2,3,1,0:T(8,128)(2,1)}, u32[]{:S(2)}, u32[]{:S(2)}) async-start(bf16[32,1,128,448]{2,3,1,0:T(8,128)(2,1)} %copy.92), calls=%async_computation.1 | async-start | bytes 7340032 | tf_op jit(solution)/shard_map/all_to_all | solution.py:41
  41.8 2.3 copy-start.9
  41.8 168.2 %all-gather.7.cloned.1.call-start = ((), (), s32[]{:S(2)}) async-start(), calls=%async_computation.4 | async-start | bytes 2162688 | tf_op jit(solution)/shard_map/all_gather | solution.py:45
  223.6 5.0 %copy-start.5 = (bf16[448,2048]{1,0:T(8,128)(2,1)S(1)}, bf16[448,2048]{1,0:T(8,128)(2,1)}, u32[]{:S(2)}) copy-start(bf16[448,2048]{1,0:T(8,128)(2,1)} %reshape.319) | copy-start | bytes 5505028
  223.6 5.0 %copy-start.12 = (bf16[12,128,448]{2,1,0:T(8,128)(2,1)S(1)}, bf16[12,128,448]{2,1,0:T(8,128)(2,1)}, u32[]{:S(2)}) copy-start(bf16[12,128,448]{2,1,0:T(8,128)(2,1)} %copy.93) | copy-start | bytes 4128772
  234.5 2.7 copy-start.2
  234.5 2.7 copy-start.13
  237.2 4.4 %copy-start.10 = (bf16[48,8,16,128]{3,2,1,0:T(8,128)(2,1)S(1)}, bf16[48,8,16,128]{3,2,1,0:T(8,128)(2,1)}, u32[]{:S(2)}) copy-start(bf16[48,8,16,128]{3,2,1,0:T(8,128)(2,1)} %copy.116) | copy-start | bytes 4718596
  237.2 11.4 %slice-start = ((s8[6291456]{0:T(1024)(128)(4,1)}), s8[2097152]{0:T(1024)(128)(4,1)S(1)}, s32[]{:S(2)}) async-start(s8[6291456]{0:T(1024)(128)(4,1)} %bitcast.111), calls=%async_computation.5 | async-start | bytes 4194304
  241.6 6.9 %slice-start.1 = ((s8[6291456]{0:T(1024)(128)(4,1)}), s8[4194304]{0:T(1024)(128)(4,1)S(1)}, s32[]{:S(2)}) async-start(s8[6291456]{0:T(1024)(128)(4,1)} %bitcast.111), calls=%async_computation.6 | async-start | bytes 8388608
  248.6 13.9 %slice-start.2 = ((s8[6291456]{0:T(1024)(128)(4,1)}), s8[2097152]{0:T(1024)(128)(4,1)S(1)}, s32[]{:S(2)}) async-start(s8[6291456]{0:T(1024)(128)(4,1)} %bitcast.115), calls=%async_computation.7 | async-start | bytes 4194304
  254.4 8.1 %slice-start.3 = ((s8[6291456]{0:T(1024)(128)(4,1)}), s8[4194304]{0:T(1024)(128)(4,1)S(1)}, s32[]{:S(2)}) async-start(s8[6291456]{0:T(1024)(128)(4,1)} %bitcast.115), calls=%async_computation.8 | async-start | bytes 8388608
  262.4 4.1 %copy-start.7 = (bf16[448,2048]{1,0:T(8,128)(2,1)S(1)}, bf16[448,2048]{1,0:T(8,128)(2,1)}, u32[]{:S(2)}) copy-start(bf16[448,2048]{1,0:T(8,128)(2,1)} %reshape.317) | copy-start | bytes 5505028
  266.5 4.7 %copy-start.3 = (bf16[6,16,64,256]{3,2,1,0:T(8,128)(2,1)S(1)}, bf16[6,16,64,256]{3,2,1,0:T(8,128)(2,1)}, u32[]{:S(2)}) copy-start(bf16[6,16,64,256]{3,2,1,0:T(8,128)(2,1)} %fusion.8) | copy-start | bytes 9437188
  273.9 4.1 %copy-start.6 = (bf16[448,2048]{1,0:T(8,128)(2,1)S(1)}, bf16[448,2048]{1,0:T(8,128)(2,1)}, u32[]{:S(2)}) copy-start(bf16[448,2048]{1,0:T(8,128)(2,1)} %reshape.319) | copy-start | bytes 5505028
  292.1 6.4 %copy-start.4 = (bf16[6,16,64,256]{3,2,1,0:T(8,128)(2,1)S(1)}, bf16[6,16,64,256]{3,2,1,0:T(8,128)(2,1)}, u32[]{:S(2)}) copy-start(bf16[6,16,64,256]{3,2,1,0:T(8,128)(2,1)} %fusion.8) | copy-start | bytes 9437188
  292.1 87.6 %all-to-all-start.2 = ((bf16[32,1,128,448]{2,3,1,0:T(8,128)(2,1)}), bf16[32,1,128,448]{2,3,1,0:T(8,128)(2,1)}, u32[]{:S(2)}, u32[]{:S(2)}) async-start(bf16[32,1,128,448]{2,3,1,0:T(8,128)(2,1)} %bitcast.108), calls=%async_computation.2 | async-start | bytes 7340032 | tf_op jit(solution)/shard_map/all_to_all | solution.py:91
  303.3 1.4 copy-start.11
  305.7 79.0 %copy-start.1 = (bf16[2,128,448]{1,2,0:T(8,128)(2,1)S(1)}, bf16[2,128,448]{1,2,0:T(8,128)(2,1)}, u32[]{:S(2)}) copy-start(bf16[2,128,448]{1,2,0:T(8,128)(2,1)} %param.10) | copy-start | bytes 688132
Sparse Core Ops, SparseCore 0:
  25.3 103.9 all-gather.4
  132.0 78.0 all-gather.6
where the time goes:
time: 396 us; the launch traced here: 392 us
  waiting for transfers between devices  243 us (61%)
  matrix products  54.4 us (14%)
  local copies, waits for them, and re-layouts  50.8 us (13%)
  starting transfers between devices  23 us (6%)
  between operations  14.6 us (4%)
  other arithmetic  6.1 us (2%)
    all_gather x1, waiting for transfers between devices, on_device(): lax.all_gather(value_weight, 'seq', axis=0, tiled=True)  84.8 us
    all_gather x1, waiting for transfers between devices, on_device(): lax.all_gather(key_weight, 'seq', axis=0, tiled=True)  76.4 us
    all_to_all x1, waiting for transfers between devices, on_device(): lax.all_to_all(outgoing_grads.reshape(peer_count, capacity, NB, E), 'seq'...  71.3 us
    unnamed x43, local copies, waits for them, and re-layouts  18.8 us
    all_to_all x1, starting transfers between devices, on_device(): lax.all_to_all(wanted, 'seq', split_axis=0, concat_axis=0, tiled=True)  11.5 us
    all_to_all x1, waiting for transfers between devices, on_device(): lax.all_to_all(wanted, 'seq', split_axis=0, concat_axis=0, tiled=True)  8.97 us
    dot_general x1, matrix products, on_device(): jnp.einsum('cihd,cthd->chit', grad_heads, value_heads, preferred_element_...  8.07 us
  transfers between devices with their start and end apart: 5, of which 4 were waited for; matrix products, arithmetic and copies ran while one was open for 6% of the time, Pallas kernels for 0%

commit v1 on v0

v1 whole, which is shorter than its diff:
```python
import functools
import math

import jax
import jax.numpy as jnp
from jax import lax
from jax.experimental import pallas as pl
from jax.experimental.pallas import tpu as pltpu
from jax.sharding import PartitionSpec as P

HEADS = 16
HDIM = 128
E = 448
SPAN = 64
NB = 128
NY = 4
NZ = 8
NX = 4
CUT = 336
REST = 448 - CUT
MIB = 1024 * 1024
MESH = pl.DeviceIdType.MESH
VM = pl.BlockSpec(memory_space=pltpu.VMEM)
SM = pl.BlockSpec(memory_space=pltpu.SMEM)


def places():
    s, b = lax.axis_index("seq"), lax.axis_index("batch")
    y, z = s // NZ, s % NZ
    x, c = b // 2, b % 2

    def at(dy, dz):
        return {"seq": ((y + dy + NY) % NY) * NZ + (z + dz + NZ) % NZ}

    dev = {
        "Y+": at(1, 0), "Y-": at(-1, 0), "YO": at(2, 0), "Z+": at(0, 1), "Z-": at(0, -1),
        "X+": {"batch": ((x + 1) % NX) * 2 + c},
        "X-": {"batch": ((x + NX - 1) % NX) * 2 + c},
        "C": {"batch": x * 2 + (1 - c)},
    }
    return y, z, x, c, dev


class Link:
    def __init__(self, dev, ssem, rsem):
        self.dev, self.ssem, self.rsem, self.all = dev, ssem, rsem, []

    def send(self, src, dst, to):
        i = len(self.all)
        cp = pltpu.make_async_remote_copy(
            src_ref=src, dst_ref=dst, send_sem=self.ssem.at[i], recv_sem=self.rsem.at[i],
            device_id=self.dev[to], device_id_type=MESH,
        )
        cp.start()
        self.all.append(cp)
        return cp

    def finish(self):
        for cp in self.all:
            cp.wait_send()


def barrier(dev, names):
    sem = pltpu.get_barrier_semaphore()
    for n in names:
        pl.semaphore_signal(sem, inc=1, device_id=dev[n], device_id_type=MESH)
    pl.semaphore_wait(sem, len(names))


def pack(x):
    tail = jnp.concatenate([x[0:64, 384:448], x[64:128, 384:448]], axis=1)
    return jnp.concatenate([x[:, 0:128], x[:, 128:256], x[:, 256:384], tail], axis=0)


def unpack(p):
    tail = jnp.concatenate([p[384:448, 0:64], p[384:448, 64:128]], axis=0)
    return jnp.concatenate([p[0:128], p[128:256], p[256:384], tail], axis=1)


N_GATHER = 124


def gather_body(asm, tab, pool, wp, r_out, wall, tabs, A, B, sbuf, relay, stab, ssem, rsem, lsem):
    y, z, x, c, dev = places()
    for j in range(2):
        pk = pack(pool[j])
        A[j] = pk[0:CUT]
        B[j] = pk[CUT:448]
    wall[0, 0, 0, 0] = wp[...]
    barrier(dev, ["Y+", "Y-", "YO", "Z+", "Z-", "X+", "X-", "C"])
    L = Link(dev, ssem, rsem)
    tcp = [
        L.send(tab, tabs.at[0], "Y+"), L.send(tab, tabs.at[1], "Y-"), L.send(tab, tabs.at[2], "YO")
    ]
    w1 = [
        L.send(wall.at[0, 0, 0, 0], wall.at[0, 0, 0, 1], "Y+"),
        L.send(wall.at[0, 0, 0, 0], wall.at[0, 0, 0, 3], "Y-"),
    ]
    b1 = [
        L.send(B.at[pl.ds(0, 2)], B.at[pl.ds(2, 2)], "Y+"),
        L.send(B.at[pl.ds(0, 2)], B.at[pl.ds(6, 2)], "Y-"),
    ]
    az = [
        L.send(A.at[pl.ds(0, 2)], A.at[pl.ds(2, 2)], "Z+"),
        L.send(A.at[pl.ds(0, 2)], A.at[pl.ds(14, 2)], "Z-"),
    ]
    for cp in w1:
        cp.wait_recv()
    w2 = [
        L.send(wall.at[0, 0, 0, 1, 0], wall.at[0, 0, 0, 2, 0], "Y+"),
        L.send(wall.at[0, 0, 0, 3, 1], wall.at[0, 0, 0, 2, 1], "Y-"),
    ]
    for cp in b1:
        cp.wait_recv()
    b2 = [
        L.send(B.at[2], B.at[4], "Y+"),
        L.send(B.at[7], B.at[5], "Y-"),
    ]
    for cp in w2:
        cp.wait_recv()
    wz = [
        L.send(wall.at[0, 0, 0], wall.at[0, 0, 1], "Z+"),
        L.send(wall.at[0, 0, 0], wall.at[0, 0, 7], "Z-"),
    ]
    core = []
    xs = {}

    def across(dz):
        xs[dz] = (
            L.send(wall.at[0, 0, dz], wall.at[1, 0, dz], "X+"),
            L.send(wall.at[0, 0, dz], wall.at[3, 0, dz], "X-"),
        )
        core.append(L.send(wall.at[0, 0, dz], wall.at[0, 1, dz], "C"))

    xf = {}

    def across_on(dz):
        for cp in xs[dz]:
            cp.wait_recv()
        if dz < 4:
            xf[dz] = L.send(wall.at[1, 0, dz], wall.at[2, 0, dz], "X+")
        else:
            xf[dz] = L.send(wall.at[3, 0, dz], wall.at[2, 0, dz], "X-")
        for k in (1, 3):
            core.append(L.send(wall.at[k, 0, dz], wall.at[k, 1, dz], "C"))

    across(0)
    for cp in tcp:
        cp.wait_recv()
    lc = [pltpu.make_async_copy(tabs.at[k], stab.at[k], lsem.at[k]) for k in range(3)]
    for cp in lc:
        cp.start()
    for cp in lc:
        cp.wait()

    direct = []
    hop = {}

    def choose(d, k, slot):
        s = stab[k, y, (z - d + NZ) % NZ]
        sbuf[slot] = lax.select(s > 0, A[2 * d + 1], A[2 * d])

    def ysend(d):
        choose(d, 1, 3 * d)
        direct.append(L.send(sbuf.at[3 * d], A.at[16 + d], "Y+"))
        choose(d, 0, 3 * d + 1)
        direct.append(L.send(sbuf.at[3 * d + 1], A.at[24 + d], "Y-"))
        choose(d, 2, 3 * d + 2)
        hop[d] = L.send(sbuf.at[3 * d + 2], relay.at[d], "Y+" if d < 4 else "Y-")

    def pass_on(d):
        hop[d].wait_recv()
        direct.append(L.send(relay.at[d], A.at[32 + d], "Y+" if d < 4 else "Y-"))

    ysend(0)
    for cp in b2:
        cp.wait_recv()
    bz = [
        L.send(B.at[pl.ds(0, 8)], B.at[pl.ds(8, 8)], "Z+"),
        L.send(B.at[pl.ds(0, 8)], B.at[pl.ds(56, 8)], "Z-"),
    ]
    for k in range(1, 4):
        m = NZ - k
        for cp in wz:
            cp.wait_recv()
        if k < 3:
            wz = [
                L.send(wall.at[0, 0, k], wall.at[0, 0, k + 1], "Z+"),
                L.send(wall.at[0, 0, m], wall.at[0, 0, m - 1], "Z-"),
            ]
        else:
            wz = [
                L.send(wall.at[0, 0, 3, pl.ds(0, 2)], wall.at[0, 0, 4, pl.ds(0, 2)], "Z+"),
                L.send(wall.at[0, 0, 5, pl.ds(2, 2)], wall.at[0, 0, 4, pl.ds(2, 2)], "Z-"),
            ]
        across(k)
        across(m)
        for cp in az:
            cp.wait_recv()
        if k < 3:
            az = [
                L.send(A.at[pl.ds(2 * k, 2)], A.at[pl.ds(2 * k + 2, 2)], "Z+"),
                L.send(A.at[pl.ds(2 * m, 2)], A.at[pl.ds(2 * m - 2, 2)], "Z-"),
            ]
        else:
            az = [L.send(A.at[6], A.at[8], "Z+"), L.send(A.at[11], A.at[9], "Z-")]
        ysend(k)
        ysend(m)
        pass_on(k - 1)
        if k > 1:
            pass_on(m + 1)
        across_on(k - 1)
        if k > 1:
            across_on(m + 1)
        for cp in bz:
            cp.wait_recv()
        if k < 3:
            bz = [
                L.send(B.at[pl.ds(8 * k, 8)], B.at[pl.ds(8 * k + 8, 8)], "Z+"),
                L.send(B.at[pl.ds(8 * m, 8)], B.at[pl.ds(8 * m - 8, 8)], "Z-"),
            ]
        else:
            bz = [
                L.send(B.at[pl.ds(24, 4)], B.at[pl.ds(32, 4)], "Z+"),
                L.send(B.at[pl.ds(44, 4)], B.at[pl.ds(36, 4)], "Z-"),
            ]
    for cp in wz:
        cp.wait_recv()
    across(4)
    for cp in az:
        cp.wait_recv()
    ysend(4)
    pass_on(3)
    pass_on(5)
    across_on(3)
    across_on(5)
    pass_on(4)
    across_on(4)
    for dz in (0, 1, 7, 2, 6, 3, 5, 4):
        xf[dz].wait_recv()
        core.append(L.send(wall.at[2, 0, dz], wall.at[2, 1, dz], "C"))
    for cp in bz:
        cp.wait_recv()
    for cp in direct:
        cp.wait_recv()
    for r in range(r_out.shape[0]):
        ia, ib = asm[r], asm[r + 16]
        r_out[r] = unpack(jnp.concatenate([A[ia], B[ib]], axis=0))
    for cp in core:
        cp.wait_recv()
    L.finish()


def gather_call(asm, tab, pool, wp, reads):
    bf = jnp.bfloat16
    return pl.pallas_call(
        gather_body,
        out_shape=(
            jax.ShapeDtypeStruct((reads, NB, E), bf),
            jax.ShapeDtypeStruct((NX, 2, NZ, NY, 2, 16, 256), bf),
            jax.ShapeDtypeStruct((3, 8, 128), jnp.int32),
        ),
        in_specs=[SM, VM, VM, VM],
        out_specs=(VM, VM, VM),
        scratch_shapes=[
            pltpu.VMEM((40, CUT, 128), bf),
            pltpu.VMEM((64, REST, 128), bf),
            pltpu.VMEM((24, CUT, 128), bf),
            pltpu.VMEM((8, CUT, 128), bf),
            pltpu.SMEM((3, 8, 128), jnp.int32),
            pltpu.SemaphoreType.DMA((N_GATHER,)),
            pltpu.SemaphoreType.DMA((N_GATHER,)),
            pltpu.SemaphoreType.DMA((3,)),
        ],
        compiler_params=pltpu.CompilerParams(
            collective_id=0, has_side_effects=True, vmem_limit_bytes=40 * MIB
        ),
        name="gather",
    )(asm, tab, pool, wp)


def nt(a, b):
    return lax.dot_general(a, b, (((1,), (1,)), ((), ())), preferred_element_type=jnp.float32)


def tn(a, b):
    return lax.dot_general(a, b, (((0,), (0,)), ((), ())), preferred_element_type=jnp.float32)


def compute_body(q, do, r, wall, bias, att, qg, rg, wk, wv, qp, op, pr, dr):
    y, z, x, c, _ = places()
    bf, f32 = jnp.bfloat16, jnp.float32
    scale = 1.0 / math.sqrt(HDIM)
    spans = r.shape[0]
    rows = spans * SPAN
    col = lax.broadcasted_iota(jnp.int32, (E, 512), 1)
    row = lax.broadcasted_iota(jnp.int32, (E, 512), 0)
    dz, dy, t = col >> 6, (col >> 4) & 3, col & 15
    source = (((y - dy) & 3) * NZ + ((z - dz) & 7)) * 14 + t
    perm = jnp.where((source == row) & (t < 14), 1.0, 0.0).astype(bf)

    def place_weight(i, _):
        dx, cc = i // 2, i % 2
        b = ((x - dx + NX) % NX) * 2 + (c + cc) % 2
        cols = pl.ds(pl.multiple_of(b * 256, 256), 256)
        for kv, w in ((0, wk), (1, wv)):
            part = wall[dx, cc, :, :, kv].reshape(512, 256)
            w[:, cols] = jnp.dot(perm, part, preferred_element_type=f32).astype(bf)
        return 0

    lax.fori_loop(0, 8, place_weight, 0)

    def project(h, _):
        cols = pl.ds(pl.multiple_of(h * HDIM, HDIM), HDIM)
        qp[:, h] = (nt(q[:, cols], wk[:, cols]) * scale).astype(bf).reshape(spans, SPAN, E)
        op[:, h] = nt(do[:, cols], wv[:, cols]).astype(bf).reshape(spans, SPAN, E)
        return 0

    lax.fori_loop(0, HEADS, project, 0)

    def span(i, _):
        rc = r[i]
        total = jnp.zeros((2 * NB, E), f32)
        for g in range(4):
            hs = pl.ds(4 * g, 4)
            qc = qp[i, hs].reshape(256, E)
            oc = op[i, hs].reshape(256, E)
            s = nt(qc, rc) + bias[hs].reshape(256, 2 * NB)
            e = jnp.exp(s - jnp.max(s, axis=-1, keepdims=True))
            p = e / jnp.sum(e, axis=-1, keepdims=True)
            low = p.astype(bf)
            pg = nt(oc, rc)
            delta = jnp.sum(low.astype(f32) * pg, axis=-1, keepdims=True)
            ds = (p * (pg - delta)).astype(bf)
            total = total + tn(ds, qc) + tn(low, oc)
            pr[i, hs] = jnp.dot(low, rc, preferred_element_type=f32).astype(bf).reshape(4, SPAN, E)
            dr[i, hs] = jnp.dot(ds, rc, preferred_element_type=f32).astype(bf).reshape(4, SPAN, E)
        low = total.astype(bf)
        rg[2 * i] = pack(low[0:NB])
        rg[2 * i + 1] = pack(low[NB:])
        return 0

    lax.fori_loop(0, spans, span, 0)
    rg[2 * spans] = jnp.zeros((448, 128), bf)

    def emit(h, _):
        cols = pl.ds(pl.multiple_of(h * HDIM, HDIM), HDIM)
        a = jnp.dot(pr[:, h].reshape(rows, E), wv[:, cols], preferred_element_type=f32)
        att[:, cols] = a.astype(bf)
        g = jnp.dot(dr[:, h].reshape(rows, E), wk[:, cols], preferred_element_type=f32)
        qg[:, cols] = (g * scale).astype(bf)
        return 0

    lax.fori_loop(0, HEADS, emit, 0)


def compute_call(q, do, r, wall, bias):
    bf = jnp.bfloat16
    spans = r.shape[0]
    stack = pltpu.VMEM((spans, HEADS, SPAN, E), bf)
    return pl.pallas_call(
        compute_body,
        out_shape=(
            jax.ShapeDtypeStruct(q.shape, bf),
            jax.ShapeDtypeStruct(q.shape, bf),
            jax.ShapeDtypeStruct((2 * spans + 1, 448, 128), bf),
        ),
        in_specs=[VM] * 5,
        out_specs=(VM, VM, VM),
        scratch_shapes=[
            pltpu.VMEM((E, HEADS * HDIM), bf), pltpu.VMEM((E, HEADS * HDIM), bf),
            stack, stack, stack, stack,
        ],
        compiler_params=pltpu.CompilerParams(vmem_limit_bytes=58 * MIB),
        name="attend",
    )(q, do, r, wall, bias)


N_RETURN = 56


def return_body(inv, tabs, rg, out, ys, yr, relay, acc, zr, D, zb, yb, ssem, rsem):
    y, z, x, c, dev = places()
    bf, f32 = jnp.bfloat16, jnp.float32
    barrier(dev, ["Y+", "Y-", "Z+", "Z-"])
    L = Link(dev, ssem, rsem)
    direct, hop = {}, {}

    def yslots(d):
        ys[3 * d] = rg[inv[8 + d], 0:CUT]
        one = L.send(ys.at[3 * d], yr.at[8 + d], "Y-")
        ys[3 * d + 1] = rg[inv[24 + d], 0:CUT]
        two = L.send(ys.at[3 * d + 1], yr.at[d], "Y+")
        ys[3 * d + 2] = rg[inv[16 + d], 0:CUT]
        hop[d] = L.send(ys.at[3 * d + 2], relay.at[d], "Y-" if d < 4 else "Y+")
        direct[d] = [one, two]

    def pass_on(d):
        hop[d].wait_recv()
        direct[d].append(L.send(relay.at[d], yr.at[16 + d], "Y-" if d < 4 else "Y+"))

    def dense(dz):
        for dy in range(NY):
            k = dy * NZ + dz
            v = rg[inv[k], CUT:448]
            s = inv[32 + k]
            zero = jnp.zeros_like(v)
            D[dz * 8 + dy * 2] = lax.select(s > 0, zero, v)
            D[dz * 8 + dy * 2 + 1] = lax.select(s > 0, v, zero)

    def row_sum(d):
        for cp in direct[d]:
            cp.wait_recv()
        zp = (z - d + NZ) % NZ
        terms = [(rg[inv[d], 0:CUT], inv[32 + d])]
        for k in range(3):
            terms.append((yr[8 * k + d], tabs[k, y, zp]))
        sums = []
        for j in range(2):
            t = None
            for v, s in terms:
                v = v.astype(f32)
                zero = jnp.zeros_like(v)
                v = lax.select(s > 0, v, zero) if j else lax.select(s > 0, zero, v)
                t = v if t is None else t + v
            sums.append(t)
        return sums

    def add_to(ref, i, n, src, k):
        for a in range(n):
            ref[i + a] = (ref[i + a].astype(f32) + src[k + a].astype(f32)).astype(bf)

    yslots(4)
    dense(4)
    bz = [
        L.send(D.at[pl.ds(32, 4)], zb.at[pl.ds(0, 4)], "Z-"),
        L.send(D.at[pl.ds(36, 4)], zb.at[pl.ds(28, 4)], "Z+"),
    ]
    yslots(3)
    yslots(5)
    dense(3)
    dense(5)
    for d in (2, 6, 1, 7, 0):
        yslots(d)
    for d in (2, 6, 1, 7, 0):
        dense(d)
    pass_on(4)
    az = []
    for k in range(3, -1, -1):
        m = NZ - k
        for cp in bz:
            cp.wait_recv()
        if k == 3:
            add_to(D, 24, 4, zb, 0)
            add_to(D, 44, 4, zb, 28)
        elif k > 0:
            add_to(D, 8 * k, 8, zb, 4 + 8 * (2 - k))
            add_to(D, 8 * m, 8, zb, 32 + 8 * (2 - k))
        if k > 0:
            at = 4 + 8 * (3 - k)
            bz = [
                L.send(D.at[pl.ds(8 * k, 8)], zb.at[pl.ds(at, 8)], "Z-"),
                L.send(D.at[pl.ds(8 * m, 8)], zb.at[pl.ds(28 + at, 8)], "Z+"),
            ]
        else:
            for a in range(8):
                t = D[a].astype(f32) + zb[20 + a].astype(f32) + zb[48 + a].astype(f32)
                D[a] = t.astype(bf)
            by = [L.send(D.at[4], yb.at[0], "Y-"), L.send(D.at[5], yb.at[3], "Y+")]
        e = k + 1
        if e == 4:
            s0, s1 = row_sum(4)
            acc[8] = s0.astype(bf)
            acc[9] = s1.astype(bf)
            az = [L.send(acc.at[8], zr.at[0], "Z-"), L.send(acc.at[9], zr.at[7], "Z+")]
        else:
            sums = {d: row_sum(d) for d in (e, NZ - e)}
            for cp in az:
                cp.wait_recv()
            at = 1 + 2 * (3 - e)
            for d, base in ((e, 0), (NZ - e, 7)):
                s0, s1 = sums[d]
                if e == 3:
                    if base == 0:
                        s0 = s0 + zr[0].astype(f32)
                    else:
                        s1 = s1 + zr[7].astype(f32)
                else:
                    s0 = s0 + zr[base + at - 2].astype(f32)
                    s1 = s1 + zr[base + at - 1].astype(f32)
                acc[2 * d] = s0.astype(bf)
                acc[2 * d + 1] = s1.astype(bf)
            f = NZ - e
            az = [
                L.send(acc.at[pl.ds(2 * e, 2)], zr.at[pl.ds(at, 2)], "Z-"),
                L.send(acc.at[pl.ds(2 * f, 2)], zr.at[pl.ds(7 + at, 2)], "Z+"),
            ]
        pass_on(k)
        if k > 0:
            pass_on(m)
    for cp in by:
        cp.wait_recv()
    add_to(D, 2, 1, yb, 0)
    add_to(D, 7, 1, yb, 3)
    by = [
        L.send(D.at[pl.ds(2, 2)], yb.at[pl.ds(1, 2)], "Y-"),
        L.send(D.at[pl.ds(6, 2)], yb.at[pl.ds(4, 2)], "Y+"),
    ]
    home = row_sum(0)
    for cp in az:
        cp.wait_recv()
    for cp in by:
        cp.wait_recv()
    for j in range(2):
        a = home[j] + zr[5 + j].astype(f32) + zr[12 + j].astype(f32)
        b = D[j].astype(f32) + yb[1 + j].astype(f32) + yb[4 + j].astype(f32)
        out[j] = unpack(jnp.concatenate([a, b], axis=0))
    L.finish()


def return_call(inv, tabs, rg):
    bf = jnp.bfloat16
    return pl.pallas_call(
        return_body,
        out_shape=jax.ShapeDtypeStruct((2, NB, E), jnp.float32),
        in_specs=[SM, SM, VM],
        out_specs=VM,
        scratch_shapes=[
            pltpu.VMEM((24, CUT, 128), bf),
            pltpu.VMEM((24, CUT, 128), bf),
            pltpu.VMEM((8, CUT, 128), bf),
            pltpu.VMEM((16, CUT, 128), bf),
            pltpu.VMEM((14, CUT, 128), bf),
            pltpu.VMEM((64, REST, 128), bf),
            pltpu.VMEM((56, REST, 128), bf),
            pltpu.VMEM((6, REST, 128), bf),
            pltpu.SemaphoreType.DMA((N_RETURN,)),
            pltpu.SemaphoreType.DMA((N_RETURN,)),
        ],
        compiler_params=pltpu.CompilerParams(
            collective_id=1, has_side_effects=True, vmem_limit_bytes=40 * MIB
        ),
        name="giveback",
    )(inv, tabs, rg)


def tables(neighbours, place):
    s = lax.axis_index("seq")
    y, z = s // NZ, s % NZ
    reads = neighbours.size
    pos = place[neighbours].reshape(reads)
    owner, j = pos // 2, pos % 2
    dy, dz = (y - owner // NZ) % NY, (z - owner % NZ) % NZ
    ia = jnp.where(dy == 0, 2 * dz + j, jnp.where(dy == 1, 16, jnp.where(dy == 3, 24, 32)) + dz)
    ib = dz * 8 + dy * 2 + j
    gap = jnp.zeros((16 - reads,), jnp.int32)
    asm = jnp.concatenate([ia, gap, ib, gap])
    own = jnp.arange(8)[:, None] * NZ + jnp.arange(128)[None, :]
    real = jnp.arange(128)[None, :] < NZ
    tab = jnp.sum(
        jnp.where((own[None] == owner[:, None, None]) & real[None], j[:, None, None], 0), axis=0
    )
    hit = (dy * NZ + dz)[:, None] == jnp.arange(32)[None, :]
    which = jnp.min(jnp.where(hit, jnp.arange(reads)[:, None], reads), axis=0)
    pick = jnp.max(jnp.where(hit, j[:, None], 0), axis=0)
    inv = jnp.concatenate([which, pick]).astype(jnp.int32)
    return asm.astype(jnp.int32), tab.astype(jnp.int32), inv


def on_device(queries, cotangent, pool, key_weight, value_weight, score_bias, neighbours, place):
    spans = queries.shape[0] // SPAN
    asm, tab, inv = tables(neighbours, place)
    b = lax.axis_index("batch")
    wp = jnp.stack([key_weight, value_weight])
    wp = lax.dynamic_slice(wp, (0, 0, b * 256), (2, 14, 256))
    wp = jnp.pad(wp, ((0, 0), (0, 2), (0, 0)))
    r, wall, tabs = gather_call(asm, tab, pool, wp, 2 * spans)
    att, qg, rg = compute_call(
        queries, cotangent, r.reshape(spans, 2 * NB, E), wall, score_bias
    )
    return att, qg, return_call(inv, tabs, rg)


def solution(mesh):
    both = ("batch", "seq")
    in_specs = (
        P(both, None), P(both, None), P(both, None, None), P("seq", None), P("seq", None),
        P(), P(both, None), P("batch"),
    )
    out_specs = (P(both, None), P(both, None), P(both, None, None))
    return jax.shard_map(
        on_device, mesh=mesh, in_specs=in_specs, out_specs=out_specs, check_vma=False
    )
```

time: 396 us -> 167 us (0.42)
  waiting for transfers between devices: 243 us -> 0 us
  Pallas kernels: 0 us -> 158 us
  matrix products: 54.4 us -> 0 us
  local copies, waits for them, and re-layouts: 50.8 us -> 6.49 us
  starting transfers between devices: 23 us -> 0 us
  between operations: 14.6 us -> 0.81 us
  other arithmetic: 6.1 us -> 1.17 us
    all_gather x2 -> x0, waiting for transfers between devices: 161 us -> none  [the longest x1 84.8 us: on_device(): lax.all_gather(value_weight, 'seq', axis=0, tiled=True)]
    pallas_call x0 -> x3, Pallas kernels: none -> 158 us  [the longest x1 58.4 us: return_call(): pl.pallas_call(return_body, out_shape=jax.ShapeDtypeStruct((2, NB, E), jn...]
    all_to_all x3 -> x0, waiting for transfers between devices: 80.3 us -> none  [the longest x1 71.3 us: on_device(): lax.all_to_all(outgoing_grads.reshape(peer_count, capacity, NB, E), 'seq'...]
    dot_general x12 -> x0, matrix products: 54.4 us -> none  [the longest x1 8.07 us: on_device(): jnp.einsum('cihd,cthd->chit', grad_heads, value_heads, preferred_element_...]
    all_to_all x3 -> x0, starting transfers between devices: 22.9 us -> none  [the longest x1 11.5 us: on_device(): lax.all_to_all(wanted, 'seq', split_axis=0, concat_axis=0, tiled=True)]
    convert_element_type x6 -> x0, local copies, waits for them, and re-layouts: 14.2 us -> none  [the longest x1 4.06 us: on_device(): key_grad = (jnp.einsum('chit,cihd->cthd', dscore_low, query_heads, prefer...]
    unnamed x43 -> x16, local copies, waits for them, and re-layouts: 18.8 us -> 5.65 us
    gather x3 -> x1, local copies, waits for them, and re-layouts: 5.72 us -> 0.66 us  [tables(): pos = place[neighbours].reshape(reads)]
  transfers between devices with their start and end apart: 5 -> 0, of which waited for: 4 -> 0; matrix products, arithmetic and copies ran while one was open for 6% -> 0% of each run, Pallas kernels for 0% -> 0%
where the time goes in v1:
time: 167 us; the launch traced here: 166 us
  Pallas kernels  158 us (95%)
  local copies, waits for them, and re-layouts  6.49 us (4%)
    pallas_call x1, Pallas kernels, return_call(): pl.pallas_call(return_body, out_shape=jax.ShapeDtypeStruct((2, NB, E), jn...  58.4 us
    pallas_call x1, Pallas kernels, gather_call(): pl.pallas_call(gather_body, out_shape=(jax.ShapeDtypeStruct((reads, NB, E...  56.7 us
    pallas_call x1, Pallas kernels, compute_call(): pl.pallas_call(compute_body, out_shape=(jax.ShapeDtypeStruct(q.shape, bf)...  42.8 us
    unnamed x16, local copies, waits for them, and re-layouts  5.65 us

profile of v1, /device:TPU:4, one launch (start us, length us, event | category | flops | bytes accessed | tf_op | source)
XLA Modules:
  0.0 166.5 jit_solution(913157043948359965)
XLA Ops:
  0.6 0.0 copy-start
  0.7 0.7 compare_select_fusion
  1.4 0.1 copy.17
  1.5 0.1 reshape.196
  1.6 0.0 copy-done
  1.6 0.0 copy-start.5
  1.6 0.0 copy-start.6
  1.6 0.0 copy-start.4
  1.6 0.7 gather_fusion
  2.3 0.1 pad_add_fusion.asm
  2.4 0.1 select_reduce_fusion.2
  2.5 0.1 pad_add_fusion.1.inv
  2.6 0.1 iota_add_fusion
  2.7 0.1 select_reduce_fusion.tab
  2.8 0.0 copy-done.5
  2.8 0.0 copy-done.6
  2.8 0.0 copy-done.4
  2.8 0.1 copy.18.pool
  3.0 56.7 %gather.7 = (bf16[12,128,448]{2,1,0:T(8,128)(2,1)S(1)}, bf16[4,2,8,4,2,16,256]{6,5,4,3,2,1,0:T(8,128)(2,1)S(1)}, s32[3,8,128]{2,1,0:T(8,128)S(1)}) custom-call(s32[32]{0:T(128)S(1)} %pad_add_fusion.asm, s32[8,128]{1,0:T(8,128)S(1)} %select_reduce_fusion.tab, bf16[2,128,448]{2,1,0:T(8,128)(2,1)S(1)} %copy.18.pool, bf16[2,16,256]{2,1,0:T(8,128)(2,1)S(1)} %pad.4.wp), custom_call_target="tpu_custom_call" | custom-call | tf_op jit(solution)/shard_map/gather/pallas_call | solution.py:256
  59.7 0.0 copy-start.1
  59.7 1.9 %copy-done.1 = bf16[4,2,8,4,2,16,256]{6,5,4,3,2,1,0:T(8,128)(2,1)} copy-done((bf16[4,2,8,4,2,16,256]{6,5,4,3,2,1,0:T(8,128)(2,1)}, bf16[4,2,8,4,2,16,256]{6,5,4,3,2,1,0:T(8,128)(2,1)S(1)}, u32[]{:S(2)}) %copy-start.1) | copy-done | bytes 4194328
  61.6 0.0 copy-start.2
  61.6 1.2 copy-done.2
  62.8 42.8 %attend.1 = (bf16[384,2048]{1,0:T(8,128)(2,1)}, bf16[384,2048]{1,0:T(8,128)(2,1)}, bf16[13,448,128]{2,1,0:T(8,128)(2,1)}) custom-call(bf16[384,2048]{1,0:T(8,128)(2,1)} %q.1, bf16[384,2048]{1,0:T(8,128)(2,1)} %do.1, bf16[6,256,448]{2,1,0:T(8,128)(2,1)} %bitcast.3, bf16[4,2,8,4,2,16,256]{6,5,4,3,2,1,0:T(8,128)(2,1)} %copy-done.1, f32[16,64,256]{2,1,0:T(8,128)} %bias.1), custom_call_target="tpu_custom_call" | custom-call | tf_op jit(solution)/shard_map/attend/pallas_call | solution.py:361
  105.7 0.0 copy-start.3
  105.7 1.4 copy-done.3
  107.0 58.4 %giveback.1 = f32[2,128,448]{2,1,0:T(8,128)S(1)} custom-call(s32[64]{0:T(128)S(1)} %pad_add_fusion.1.inv, s32[3,8,128]{2,1,0:T(8,128)S(1)} %get-tuple-element.13.tabs, bf16[13,448,128]{2,1,0:T(8,128)(2,1)S(1)} %copy-done.3), custom_call_target="tpu_custom_call" | custom-call | tf_op jit(solution)/shard_map/giveback/pallas_call | solution.py:523
  165.5 1.0 copy.19
  (9 shorter events, 0.1 us)
Async XLA Ops:
  0.6 0.9 copy-start
  1.6 1.2 copy-start.5
  1.6 1.2 copy-start.6
  1.6 1.2 copy-start.4
  59.7 1.9 %copy-start.1 = (bf16[4,2,8,4,2,16,256]{6,5,4,3,2,1,0:T(8,128)(2,1)}, bf16[4,2,8,4,2,16,256]{6,5,4,3,2,1,0:T(8,128)(2,1)S(1)}, u32[]{:S(2)}) copy-start(bf16[4,2,8,4,2,16,256]{6,5,4,3,2,1,0:T(8,128)(2,1)S(1)} %get-tuple-element.10.wall) | copy-start | bytes 12582916
  61.6 1.2 copy-start.2
  105.7 1.4 copy-start.3

commit v2 on v0

v2 whole, which is shorter than its diff:
```python
import functools
import math

import jax
import jax.numpy as jnp
from jax import lax
from jax.experimental import pallas as pl
from jax.experimental.pallas import tpu as pltpu
from jax.sharding import PartitionSpec as P

HEADS = 16
HDIM = 128
E = 448
SPAN = 64
NB = 128
NY = 4
NZ = 8
NX = 4
LOW = 240
TOP = 448 - LOW
LOW2 = 304
TOP2 = 448 - LOW2
MIB = 1024 * 1024
VMEM_ASK = 63 * MIB
MESH = pl.DeviceIdType.MESH
VM = pl.BlockSpec(memory_space=pltpu.VMEM)
SM = pl.BlockSpec(memory_space=pltpu.SMEM)


def places():
    s, b = lax.axis_index("seq"), lax.axis_index("batch")
    y, z = s // NZ, s % NZ
    x, c = b // 2, b % 2

    def at(dy, dz):
        return {"seq": ((y + dy + NY) % NY) * NZ + (z + dz + NZ) % NZ}

    dev = {
        "Y+": at(1, 0), "Y-": at(-1, 0), "YO": at(2, 0), "Z+": at(0, 1), "Z-": at(0, -1),
        "X+": {"batch": ((x + 1) % NX) * 2 + c},
        "X-": {"batch": ((x + NX - 1) % NX) * 2 + c},
        "C": {"batch": x * 2 + (1 - c)},
    }
    return y, z, x, c, dev


class Link:
    def __init__(self, dev, ssem, rsem):
        self.dev, self.ssem, self.rsem, self.n, self.all = dev, ssem, rsem, 0, []

    def send(self, src, dst, to):
        i, self.n = self.n, self.n + 1
        cp = pltpu.make_async_remote_copy(
            src_ref=src, dst_ref=dst, send_sem=self.ssem.at[i], recv_sem=self.rsem.at[i],
            device_id=self.dev[to], device_id_type=MESH,
        )
        cp.start()
        self.all.append(cp)
        return cp

    def finish(self):
        for cp in self.all:
            cp.wait_send()
        self.all = []


def barrier(dev, names):
    sem = pltpu.get_barrier_semaphore()
    for n in names:
        pl.semaphore_signal(sem, inc=1, device_id=dev[n], device_id_type=MESH)
    pl.semaphore_wait(sem, len(names))


def pack(x):
    tail = jnp.concatenate([x[0:64, 384:448], x[64:128, 384:448]], axis=1)
    return jnp.concatenate([x[:, 0:128], x[:, 128:256], x[:, 256:384], tail], axis=0)


def unpack(p):
    tail = jnp.concatenate([p[384:448, 0:64], p[384:448, 64:128]], axis=0)
    return jnp.concatenate([p[0:128], p[128:256], p[256:384], tail], axis=1)


def nt(a, b):
    return lax.dot_general(a, b, (((1,), (1,)), ((), ())), preferred_element_type=jnp.float32)


def tn(a, b):
    return lax.dot_general(a, b, (((0,), (0,)), ((), ())), preferred_element_type=jnp.float32)


N_COPIES = 168


def body(asm, inv, tab, pool, wp, q_hbm, do_hbm, bias_hbm, att_hbm, qg_hbm, out,
         q, do, bias, bias_t, wall, perm, wk, wv, qo, pp, r, tabs, stab, F, O, sb, sbo, rg,
         yr, yro, yso, acc, oc, zr, zo, of, ssem, rsem, lsem):
    y, z, x, c, dev = places()
    bf, f32 = jnp.bfloat16, jnp.float32
    scale = 1.0 / math.sqrt(HDIM)
    spans = r.shape[0]
    rows = spans * SPAN
    loads = [
        pltpu.make_async_copy(a, b, lsem.at[i])
        for i, (a, b) in enumerate(((bias_hbm, bias), (q_hbm, q), (do_hbm, do)))
    ]
    for cp in loads:
        cp.start()
    for j in range(2):
        F[j] = pack(pool[j])
    wall[0, 0, 0, 0] = wp[...]
    barrier(dev, ["Y+", "Y-", "YO", "Z+", "Z-", "X+", "X-", "C"])
    L = Link(dev, ssem, rsem)

    def got(cps):
        for cp in cps:
            cp.wait_recv()

    tcp = [
        L.send(tab, tabs.at[0], "Y+"), L.send(tab, tabs.at[1], "Y-"), L.send(tab, tabs.at[2], "YO")
    ]
    w1 = [
        L.send(wall.at[0, 0, 0, 0], wall.at[0, 0, 0, 1], "Y+"),
        L.send(wall.at[0, 0, 0, 0], wall.at[0, 0, 0, 3], "Y-"),
        L.send(wall.at[0, 0, 0, 0], wall.at[0, 0, 0, 2], "YO"),
    ]

    def own(k, j):
        a, b = k - 1, (NZ - k + 1) % NZ
        cps = []
        if k < 4 or j == 0:
            cps.append(L.send(F.at[2 * a + j], F.at[2 * k + j], "Z+"))
        if k < 4 or j == 1:
            cps.append(L.send(F.at[2 * b + j], F.at[2 * (NZ - k) + j], "Z-"))
        return cps

    def opp(k):
        a, b, m = k - 1, (NZ - k + 1) % NZ, NZ - k
        if k == 4:
            return [L.send(O.at[6], O.at[8], "Z+"), L.send(O.at[11], O.at[9], "Z-")]
        return [
            L.send(O.at[pl.ds(2 * a, 2)], O.at[pl.ds(2 * k, 2)], "Z+"),
            L.send(O.at[pl.ds(2 * b, 2)], O.at[pl.ds(2 * m, 2)], "Z-"),
        ]

    def weights(k):
        a, b, m = k - 1, (NZ - k + 1) % NZ, NZ - k
        if k == 4:
            return [
                L.send(wall.at[0, 0, 3, pl.ds(0, 2)], wall.at[0, 0, 4, pl.ds(0, 2)], "Z+"),
                L.send(wall.at[0, 0, 5, pl.ds(2, 2)], wall.at[0, 0, 4, pl.ds(2, 2)], "Z-"),
            ]
        return [
            L.send(wall.at[0, 0, a], wall.at[0, 0, k], "Z+"),
            L.send(wall.at[0, 0, b], wall.at[0, 0, m], "Z-"),
        ]

    core, xs, xf = {}, {}, {}

    def to_core(dx, dz):
        core[dx, dz] = L.send(wall.at[dx, 0, dz], wall.at[dx, 1, dz], "C")

    def across(dz):
        xs[dz] = (
            L.send(wall.at[0, 0, dz], wall.at[1, 0, dz], "X+"),
            L.send(wall.at[0, 0, dz], wall.at[3, 0, dz], "X-"),
        )
        to_core(0, dz)

    def across_on(dz):
        got(xs[dz])
        if dz < 4:
            xf[dz] = L.send(wall.at[1, 0, dz], wall.at[2, 0, dz], "X+")
        else:
            xf[dz] = L.send(wall.at[3, 0, dz], wall.at[2, 0, dz], "X-")
        to_core(1, dz)
        to_core(3, dz)

    direct = []

    def ysend(d):
        zp = (z - d + NZ) % NZ
        sb[2 * d] = lax.select(stab[1, y, zp] > 0, F[2 * d + 1], F[2 * d])
        direct.append(L.send(sb.at[2 * d], F.at[16 + d], "Y+"))
        sb[2 * d + 1] = lax.select(stab[0, y, zp] > 0, F[2 * d + 1], F[2 * d])
        direct.append(L.send(sb.at[2 * d + 1], F.at[24 + d], "Y-"))
        sbo[d] = lax.select(stab[2, y, zp] > 0, F[2 * d + 1, 0:TOP], F[2 * d, 0:TOP])
        direct.append(L.send(sbo.at[d], F.at[32 + d, pl.ds(0, TOP)], "YO"))

    def project(dx, cc):
        if cc:
            got([core[dx, dz] for dz in range(NZ)])
        b = ((x - dx + NX) % NX) * 2 + (c + cc) % 2
        wide = pl.ds(pl.multiple_of(b * 256, 256), 256)
        pm = perm[...]
        for kv, w, src, base in ((0, wk, q, 0), (1, wv, do, HEADS * SPAN)):
            part = wall[dx, cc, :, :, kv].reshape(512, 256)
            wb = jnp.dot(pm, part, preferred_element_type=f32).astype(bf)
            w[:, wide] = wb
            rows_in = src[:, wide]
            for hh in range(2):
                t = nt(rows_in[:, hh * HDIM:(hh + 1) * HDIM], wb[:, hh * HDIM:(hh + 1) * HDIM])
                if kv == 0:
                    t = t * scale
                at = pl.ds(pl.multiple_of(base + b * 128 + hh * SPAN, SPAN), SPAN)
                qo[:, at] = t.astype(bf).reshape(spans, SPAN, E)

    o1 = [own(1, 0)]
    ex = L.send(F.at[pl.ds(0, 2), pl.ds(TOP, LOW)], O.at[pl.ds(0, 2)], "YO")
    got(w1)
    wz = weights(1)
    o1.append(own(1, 1))
    across(0)
    got(tcp)
    lc = [pltpu.make_async_copy(tabs.at[k], stab.at[k], lsem.at[3 + k]) for k in range(3)]
    for cp in lc:
        cp.start()
    for cp in lc:
        cp.wait()
    ysend(0)
    col = lax.broadcasted_iota(jnp.int32, (E, 512), 1)
    row = lax.broadcasted_iota(jnp.int32, (E, 512), 0)
    dz, dy, t = col >> 6, (col >> 4) & 3, col & 15
    source = (((y - dy) & 3) * NZ + ((z - dz) & 7)) * 14 + t
    perm[...] = jnp.where((source == row) & (t < 14), 1.0, 0.0).astype(bf)
    got(o1[0])
    o2 = [own(2, 0)]
    got(wz)
    wz = weights(2)
    across(1)
    across(7)
    got(o1[1])
    o2.append(own(2, 1))
    ysend(1)
    ysend(7)
    got([ex])
    oz = opp(1)
    got(wz)
    wz = weights(3)
    across(2)
    across(6)
    across_on(0)
    loads[0].wait()
    bias_t[...] = bias[...].T
    got(o2[0])
    o3 = [own(3, 0)]
    got(wz)
    wz = weights(4)
    across(3)
    across(5)
    got(o2[1])
    o3.append(own(3, 1))
    ysend(2)
    ysend(6)
    across_on(1)
    across_on(7)
    got(oz)
    oz = opp(2)
    got(wz)
    across(4)
    across_on(2)
    across_on(6)
    loads[1].wait()
    loads[2].wait()
    project(0, 0)
    got(o3[0])
    o4 = own(4, 0)
    got(o3[1])
    o4 = o4 + own(4, 1)
    ysend(3)
    ysend(5)
    across_on(3)
    across_on(5)
    got(oz)
    oz = opp(3)
    across_on(4)
    project(0, 1)
    project(1, 0)
    got(o4)
    ysend(4)
    for d in range(NZ):
        xf[d].wait_recv()
        to_core(2, d)
    project(3, 0)
    got(oz)
    oz = opp(4)
    project(1, 1)
    project(3, 1)
    project(2, 0)
    project(2, 1)
    got(oz)
    got(direct)
    for d in range(NZ):
        F[32 + d, TOP:448] = lax.select(inv[48 + d] > 0, O[2 * d + 1], O[2 * d])
    for i in range(spans):
        for j in range(2):
            r[i, j * NB:(j + 1) * NB] = unpack(F[asm[2 * i + j]])
    L.finish()

    half = HEADS * SPAN

    def stage1(i):
        return nt(r[i], qo[i, 0:half]) + bias_t[...], nt(r[i], qo[i, half:])

    def stage2(i, s, pg):
        e = jnp.exp(s - jnp.max(s, axis=0, keepdims=True))
        p = e * (1.0 / jnp.sum(e, axis=0, keepdims=True))
        low = p.astype(bf)
        delta = jnp.sum(low.astype(f32) * pg, axis=0, keepdims=True)
        ds = (p * (pg - delta)).astype(bf)
        pp[i, :, 0:half] = ds
        pp[i, :, half:] = low
        return ds, low

    def stage3(i, ds, low):
        g = jnp.dot(ds, qo[i, 0:half], preferred_element_type=f32)
        g = (g + jnp.dot(low, qo[i, half:], preferred_element_type=f32)).astype(bf)
        rg[2 * i] = pack(g[0:NB])
        rg[2 * i + 1] = pack(g[NB:])

    ahead, behind = stage1(0), None
    for i in range(spans):
        later = stage1(i + 1) if i + 1 < spans else None
        now = stage2(i, *ahead)
        if behind is not None:
            stage3(i - 1, *behind)
        ahead, behind = later, now
    stage3(spans - 1, *behind)
    rg[2 * spans] = jnp.zeros((448, 128), bf)

    back = {}

    def yslots(d):
        sb[2 * d] = rg[inv[8 + d]]
        one = L.send(sb.at[2 * d], yr.at[8 + d], "Y-")
        sb[2 * d + 1] = rg[inv[24 + d]]
        two = L.send(sb.at[2 * d + 1], yr.at[d], "Y+")
        yso[d] = rg[inv[16 + d], 0:TOP2]
        back[d] = [one, two, L.send(yso.at[d], yro.at[d], "YO")]

    def dense(d):
        v = rg[inv[16 + d], TOP2:448]
        s = inv[48 + d]
        zero = jnp.zeros_like(v)
        oc[2 * d] = lax.select(s > 0, zero, v)
        oc[2 * d + 1] = lax.select(s > 0, v, zero)

    def pick(terms, j):
        t = None
        for v, s in terms:
            v = v.astype(f32)
            zero = jnp.zeros_like(v)
            v = lax.select(s > 0, v, zero) if j else lax.select(s > 0, zero, v)
            t = v if t is None else t + v
        return t

    def row_sum(d, j):
        zp = (z - d + NZ) % NZ
        s0, s1, s2 = tabs_at(0, zp), tabs_at(1, zp), tabs_at(2, zp)
        mine = rg[inv[d]]
        near = [(mine, inv[32 + d]), (yr[d], s0), (yr[8 + d], s1)]
        top = [(v[0:TOP2], s) for v, s in near] + [(yro[d], s2)]
        return pick(top, j), pick([(v[TOP2:448], s) for v, s in near], j)

    def tabs_at(k, zp):
        return stab[k, y, zp]

    def add_block(d, j, extra):
        top, low = row_sum(d, j)
        for ref in extra:
            top = top + ref[0:TOP2].astype(f32)
            low = low + ref[TOP2:448].astype(f32)
        return top, low

    group = 4 * SPAN
    outs = []

    def mix(g, base):
        for i in range(spans):
            t = tn(pp[i, :, base + g * group:base + (g + 1) * group], r[i])
            qo[i, base + g * group:base + (g + 1) * group] = t.astype(bf)

    def emit(g, base, w, dst, hbm, k):
        for h in range(4 * g, 4 * g + 4):
            v = qo[:, base + h * SPAN:base + (h + 1) * SPAN].reshape(rows, E)
            t = jnp.dot(v, w[:, h * HDIM:(h + 1) * HDIM], preferred_element_type=f32)
            if k == 1:
                t = t * scale
            dst[:, h * HDIM:(h + 1) * HDIM] = t.astype(bf)
        cols = pl.ds(4 * g * HDIM, 4 * HDIM)
        cp = pltpu.make_async_copy(dst.at[:, cols], hbm.at[:, cols], lsem.at[6 + 2 * g + k])
        cp.start()
        outs.append(cp)

    tasks = []
    for g in range(4):
        tasks.append(functools.partial(mix, g, half))
        tasks.append(functools.partial(emit, g, half, wv, q, att_hbm, 0))
        tasks.append(functools.partial(mix, g, 0))
        tasks.append(functools.partial(emit, g, 0, wk, do, qg_hbm, 1))

    def work(n):
        for _ in range(n):
            if tasks:
                tasks.pop(0)()

    def add_to(ref, i, n, src, k):
        for a in range(n):
            ref[i + a] = (ref[i + a].astype(f32) + src[k + a].astype(f32)).astype(bf)

    yslots(4)
    dense(4)
    oz = [L.send(oc.at[8], zo.at[0], "Z-"), L.send(oc.at[9], zo.at[7], "Z+")]
    yslots(3)
    yslots(5)
    dense(3)
    dense(5)
    yslots(2)
    yslots(6)
    yslots(1)
    yslots(7)
    yslots(0)
    for d in (2, 6, 1, 7, 0):
        dense(d)

    def own_back(e, prev):
        if e == 4:
            got(back[4])
            cps = []
            for j, to, at in ((0, "Z-", 0), (1, "Z+", 7)):
                top, low = row_sum(4, j)
                acc[8 + j, 0:TOP2] = top.astype(bf)
                acc[8 + j, TOP2:448] = low.astype(bf)
                cps.append(L.send(acc.at[8 + j], zr.at[at], to))
            return cps
        f = NZ - e
        got(back[e])
        got(back[f])
        at = 1 + 2 * (3 - e)
        cps = []
        for j in range(2):
            for d, base, to in ((e, 0, "Z-"), (f, 7, "Z+")):
                extra = []
                if e == 3:
                    if (j == 0) == (base == 0):
                        prev[base // 7].wait_recv()
                        extra = [zr.at[base]]
                else:
                    prev[2 * j + base // 7].wait_recv()
                    extra = [zr.at[base + at - 2 + j]]
                top, low = add_block(d, j, extra)
                acc[2 * d + j, 0:TOP2] = top.astype(bf)
                acc[2 * d + j, TOP2:448] = low.astype(bf)
                cps.append(L.send(acc.at[2 * d + j], zr.at[base + at + j], to))
        return cps

    def opp_back(e):
        got(oz)
        f = NZ - e
        if e == 3:
            add_to(oc, 6, 1, zo, 0)
            add_to(oc, 11, 1, zo, 7)
        elif e > 0:
            add_to(oc, 2 * e, 2, zo, 1 + 2 * (2 - e))
            add_to(oc, 2 * f, 2, zo, 8 + 2 * (2 - e))
        else:
            for j in range(2):
                t = oc[j].astype(f32) + zo[5 + j].astype(f32) + zo[12 + j].astype(f32)
                oc[j] = t.astype(bf)
            return [L.send(oc.at[pl.ds(0, 2)], of, "YO")]
        at = 1 + 2 * (3 - e)
        return [
            L.send(oc.at[pl.ds(2 * e, 2)], zo.at[pl.ds(at, 2)], "Z-"),
            L.send(oc.at[pl.ds(2 * f, 2)], zo.at[pl.ds(7 + at, 2)], "Z+"),
        ]

    work(1)
    oz = opp_back(3)
    work(1)
    oy = own_back(4, None)
    work(2)
    oz = opp_back(2)
    work(2)
    oy = own_back(3, oy)
    work(2)
    oz = opp_back(1)
    work(3)
    oy = own_back(2, oy)
    work(2)
    oz = opp_back(0)
    work(2)
    oy = own_back(1, oy)
    work(16)
    got(back[0])
    for j in range(2):
        got(oy[2 * j:2 * j + 2])
        if j == 0:
            got(oz)
        top, low = add_block(0, j, [zr.at[5 + j], zr.at[12 + j]])
        low = low + of[j].astype(f32)
        out[j] = unpack(jnp.concatenate([top, low], axis=0))
    for cp in outs:
        cp.wait()
    L.finish()


def call(asm, inv, tab, pool, wp, q, do, bias):
    bf, f32 = jnp.bfloat16, jnp.float32
    rows = q.shape[0]
    spans = rows // SPAN
    sizes = (
        ((rows, 2048), bf), ((rows, 2048), bf),
        ((HEADS * SPAN, 256), f32), ((256, HEADS * SPAN), f32),
        ((NX, 2, NZ, NY, 2, 16, 256), bf), ((E, 512), bf),
        ((E, 2048), bf), ((E, 2048), bf),
        ((spans, 2 * HEADS * SPAN, E), bf), ((spans, 256, 2 * HEADS * SPAN), bf),
        ((spans, 256, E), bf), ((3, 8, 128), jnp.int32), None,
        ((40, 448, 128), bf), ((16, LOW, 128), bf),
        ((16, 448, 128), bf), ((8, TOP, 128), bf), ((2 * spans + 1, 448, 128), bf),
        ((16, 448, 128), bf), ((8, TOP2, 128), bf), ((8, TOP2, 128), bf),
        ((16, 448, 128), bf), ((16, LOW2, 128), bf),
        ((14, 448, 128), bf), ((14, LOW2, 128), bf), ((2, LOW2, 128), bf),
    )
    scratch = [
        pltpu.SMEM((3, 8, 128), jnp.int32) if s is None else pltpu.VMEM(*s) for s in sizes
    ]
    scratch += [
        pltpu.SemaphoreType.DMA((N_COPIES,)), pltpu.SemaphoreType.DMA((N_COPIES,)),
        pltpu.SemaphoreType.DMA((14,)),
    ]
    hbm = pl.BlockSpec(memory_space=pl.ANY)
    return pl.pallas_call(
        body,
        out_shape=(
            jax.ShapeDtypeStruct(q.shape, bf),
            jax.ShapeDtypeStruct(q.shape, bf),
            jax.ShapeDtypeStruct((2, NB, E), f32),
        ),
        in_specs=[SM, SM, VM, VM, VM, hbm, hbm, hbm],
        out_specs=(hbm, hbm, VM),
        scratch_shapes=scratch,
        compiler_params=pltpu.CompilerParams(
            collective_id=0, has_side_effects=True, vmem_limit_bytes=VMEM_ASK
        ),
        name="retro",
    )(asm, inv, tab, pool, wp, q, do, bias)


def tables(neighbours, place):
    s = lax.axis_index("seq")
    y, z = s // NZ, s % NZ
    reads = neighbours.size
    pos = place[neighbours].reshape(reads)
    owner, j = pos // 2, pos % 2
    dy, dz = (y - owner // NZ) % NY, (z - owner % NZ) % NZ
    ia = jnp.where(dy == 0, 2 * dz + j, jnp.where(dy == 1, 16, jnp.where(dy == 3, 24, 32)) + dz)
    gap = jnp.zeros((16 - reads,), jnp.int32)
    asm = jnp.concatenate([ia, gap])
    own = jnp.arange(8)[:, None] * NZ + jnp.arange(128)[None, :]
    real = jnp.arange(128)[None, :] < NZ
    tab = jnp.sum(
        jnp.where((own[None] == owner[:, None, None]) & real[None], j[:, None, None], 0), axis=0
    )
    hit = (dy * NZ + dz)[:, None] == jnp.arange(32)[None, :]
    which = jnp.min(jnp.where(hit, jnp.arange(reads)[:, None], reads), axis=0)
    pick = jnp.max(jnp.where(hit, j[:, None], 0), axis=0)
    inv = jnp.concatenate([which, pick]).astype(jnp.int32)
    return asm.astype(jnp.int32), tab.astype(jnp.int32), inv


def on_device(queries, cotangent, pool, key_weight, value_weight, score_bias, neighbours, place):
    asm, tab, inv = tables(neighbours, place)
    b = lax.axis_index("batch")
    wp = jnp.stack([key_weight, value_weight])
    wp = lax.dynamic_slice(wp, (0, 0, b * 256), (2, 14, 256))
    wp = jnp.pad(wp, ((0, 0), (0, 2), (0, 0)))
    bias = score_bias.reshape(HEADS * SPAN, 2 * NB)
    return call(asm, inv, tab, pool, wp, queries, cotangent, bias)


def solution(mesh):
    both = ("batch", "seq")
    in_specs = (
        P(both, None), P(both, None), P(both, None, None), P("seq", None), P("seq", None),
        P(), P(both, None), P("batch"),
    )
    out_specs = (P(both, None), P(both, None), P(both, None, None))
    return jax.shard_map(
        on_device, mesh=mesh, in_specs=in_specs, out_specs=out_specs, check_vma=False
    )
```

time: 396 us -> 106 us (0.27); the launches traced: 392 us -> 106 us
  waiting for transfers between devices: 243 us -> 0 us
  Pallas kernels: 0 us -> 94.3 us
  matrix products: 54.4 us -> 0 us
  local copies, waits for them, and re-layouts: 50.8 us -> 8.92 us
  starting transfers between devices: 23 us -> 0 us
  between operations: 14.6 us -> 0.74 us
    all_gather x2 -> x0, waiting for transfers between devices: 161 us -> none  [the longest x1 84.8 us: on_device(): lax.all_gather(value_weight, 'seq', axis=0, tiled=True)]
    pallas_call x0 -> x1, Pallas kernels: none -> 94.3 us  [call(): pl.pallas_call(body, out_shape=(jax.ShapeDtypeStruct(q.shape, bf), jax.Sh...]
    all_to_all x3 -> x0, waiting for transfers between devices: 80.3 us -> none  [the longest x1 71.3 us: on_device(): lax.all_to_all(outgoing_grads.reshape(peer_count, capacity, NB, E), 'seq'...]
    dot_general x12 -> x0, matrix products: 54.4 us -> none  [the longest x1 8.07 us: on_device(): jnp.einsum('cihd,cthd->chit', grad_heads, value_heads, preferred_element_...]
    all_to_all x3 -> x0, starting transfers between devices: 22.9 us -> none  [the longest x1 11.5 us: on_device(): lax.all_to_all(wanted, 'seq', split_axis=0, concat_axis=0, tiled=True)]
    convert_element_type x6 -> x0, local copies, waits for them, and re-layouts: 14.2 us -> none  [the longest x1 4.06 us: on_device(): key_grad = (jnp.einsum('chit,cihd->cthd', dscore_low, query_heads, prefer...]
    unnamed x43 -> x13, local copies, waits for them, and re-layouts: 18.8 us -> 4.87 us
    gather x3 -> x1, local copies, waits for them, and re-layouts: 5.72 us -> 0.66 us  [tables(): pos = place[neighbours].reshape(reads)]
  transfers between devices with their start and end apart: 5 -> 0, of which waited for: 4 -> 0; matrix products, arithmetic and copies ran while one was open for 6% -> 0% of each run, Pallas kernels for 0% -> 0%
where the time goes in v2:
time: 106 us
  Pallas kernels  94.3 us (89%)
  local copies, waits for them, and re-layouts  8.92 us (8%)
  other arithmetic  2.26 us (2%)
    pallas_call x1, Pallas kernels, call(): pl.pallas_call(body, out_shape=(jax.ShapeDtypeStruct(q.shape, bf), jax.Sh...  94.3 us
    unnamed x13, local copies, waits for them, and re-layouts  4.87 us

profile of v2, /device:TPU:4, one launch (start us, length us, event | category | flops | bytes accessed | tf_op | source)
XLA Modules:
  0.0 106.2 jit_solution(4267318296239725530)
XLA Ops:
  0.6 0.0 copy-start
  0.7 0.7 compare_select_fusion
  1.4 0.1 copy.17
  1.5 0.1 reshape.196
  1.6 0.0 copy-done
  1.6 0.0 copy-start.3
  1.6 0.0 copy-start.4
  1.6 0.0 copy-start.2
  1.6 0.7 gather_fusion
  2.3 0.6 concatenate.6.asm
  2.9 0.1 select_reduce_fusion.2
  3.0 0.7 pad_add_fusion.inv
  3.7 0.1 iota_add_fusion
  3.7 0.7 select_reduce_fusion.tab
  4.4 0.0 copy-done.3
  4.4 0.0 copy-done.4
  4.4 0.6 pad.5.wp
  5.0 0.0 copy-done.2
  5.1 0.9 copy.18.pool
  5.9 94.3 %retro.1 = (bf16[384,2048]{1,0:T(8,128)(2,1)}, bf16[384,2048]{1,0:T(8,128)(2,1)}, f32[2,128,448]{2,1,0:T(8,128)}) custom-call(s32[16]{0:T(128)} %concatenate.6.asm, s32[64]{0:T(128)} %pad_add_fusion.inv, s32[8,128]{1,0:T(8,128)} %select_reduce_fusion.tab, bf16[2,128,448]{2,1,0:T(8,128)(2,1)} %copy.18.pool, bf16[2,16,256]{2,1,0:T(8,128)(2,1)} %pad.5.wp, ...), custom_call_target="tpu_custom_call" | custom-call | tf_op jit(solution)/shard_map/retro/pallas_call | solution.py:532
  100.2 2.0 %copy.19 = f32[2,128,448]{1,2,0:T(8,128)} copy(f32[2,128,448]{2,1,0:T(8,128)} %get-tuple-element.11) | data formatting | bytes 917504 | tf_op jit(solution)/shard_map/retro/pallas_call | solution.py:532
  102.2 0.0 copy-start.1
  102.2 2.8 %copy.22 = bf16[384,2048]{1,0:T(8,128)(2,1)} copy(bf16[384,2048]{1,0:T(8,128)(2,1)} %get-tuple-element.23) | data formatting | bytes 3145728
  105.0 0.0 copy-done.1
  105.0 1.1 %copy.23 = bf16[384,2048]{1,0:T(8,128)(2,1)} copy(bf16[384,2048]{1,0:T(8,128)(2,1)S(1)} %copy-done.1) | data formatting | bytes 3145728
  (6 shorter events, 0.1 us)
Async XLA Ops:
  0.6 0.9 copy-start
  1.6 2.9 %copy-start.3 = (bf16[14,2048]{1,0:T(8,128)(2,1)S(1)}, bf16[14,2048]{1,0:T(8,128)(2,1)}, u32[]{:S(2)}) copy-start(bf16[14,2048]{1,0:T(8,128)(2,1)} %param.11) | copy-start | bytes 172036
  1.6 2.8 %copy-start.4 = (bf16[14,2048]{1,0:T(8,128)(2,1)S(1)}, bf16[14,2048]{1,0:T(8,128)(2,1)}, u32[]{:S(2)}) copy-start(bf16[14,2048]{1,0:T(8,128)(2,1)} %param.12) | copy-start | bytes 172036
  1.6 3.5 %copy-start.2 = (bf16[2,128,448]{1,2,0:T(8,128)(2,1)S(1)}, bf16[2,128,448]{1,2,0:T(8,128)(2,1)}, u32[]{:S(2)}) copy-start(bf16[2,128,448]{1,2,0:T(8,128)(2,1)} %param.10) | copy-start | bytes 688132
  102.2 2.9 %copy-start.1 = (bf16[384,2048]{1,0:T(8,128)(2,1)S(1)}, bf16[384,2048]{1,0:T(8,128)(2,1)}, u32[]{:S(2)}) copy-start(bf16[384,2048]{1,0:T(8,128)(2,1)} %get-tuple-element.24) | copy-start | bytes 4718596

commit v3 on v2

v3 whole, which is shorter than its diff:
```python
import functools
import math

import jax
import jax.numpy as jnp
from jax import lax
from jax.experimental import pallas as pl
from jax.experimental.pallas import tpu as pltpu
from jax.sharding import PartitionSpec as P

HEADS = 16
HDIM = 128
E = 448
SPAN = 64
NB = 128
NY = 4
NZ = 8
NX = 4
LOW = 208
TOP = 448 - LOW
LOW2 = 272
TOP2 = 448 - LOW2
MIB = 1024 * 1024
VMEM_ASK = 63 * MIB
MESH = pl.DeviceIdType.MESH
VM = pl.BlockSpec(memory_space=pltpu.VMEM)
SM = pl.BlockSpec(memory_space=pltpu.SMEM)


def places():
    s, b = lax.axis_index("seq"), lax.axis_index("batch")
    y, z = s // NZ, s % NZ
    x, c = b // 2, b % 2

    def at(dy, dz):
        return {"seq": ((y + dy + NY) % NY) * NZ + (z + dz + NZ) % NZ}

    dev = {
        "Y+": at(1, 0), "Y-": at(-1, 0), "YO": at(2, 0), "Z+": at(0, 1), "Z-": at(0, -1),
        "X+": {"batch": ((x + 1) % NX) * 2 + c},
        "X-": {"batch": ((x + NX - 1) % NX) * 2 + c},
        "C": {"batch": x * 2 + (1 - c)},
    }
    return y, z, x, c, dev


class Link:
    def __init__(self, dev, ssem, rsem):
        self.dev, self.ssem, self.rsem, self.n, self.kinds, self.sent = dev, ssem, rsem, 0, {}, {}

    def group(self):
        self.n += 1
        return self.n - 1

    def send(self, src, dst, to, kind, group=None):
        at = self.kinds.setdefault(kind, len(self.kinds))
        self.sent[kind] = self.sent.get(kind, 0) + math.prod(src.shape)
        cp = pltpu.make_async_remote_copy(
            src_ref=src, dst_ref=dst, send_sem=self.ssem.at[at],
            recv_sem=self.rsem.at[self.group() if group is None else group],
            device_id=self.dev[to], device_id_type=MESH,
        )
        cp.start()
        return cp

    def landed(self, ref, group):
        pltpu.make_async_copy(ref, ref, self.rsem.at[group]).wait()

    def gone(self, ref, kind):
        assert math.prod(ref.shape) == self.sent.pop(kind), kind
        pltpu.make_async_copy(ref, ref, self.ssem.at[self.kinds[kind]]).wait()


def barrier(dev, names):
    sem = pltpu.get_barrier_semaphore()
    for n in names:
        pl.semaphore_signal(sem, inc=1, device_id=dev[n], device_id_type=MESH)
    pl.semaphore_wait(sem, len(names))


def nt(a, b):
    return lax.dot_general(a, b, (((1,), (1,)), ((), ())), preferred_element_type=jnp.float32)


def tn(a, b):
    return lax.dot_general(a, b, (((0,), (0,)), ((), ())), preferred_element_type=jnp.float32)


N_LANDING = 93
N_LEAVING = 10


def body(place, near, pool, kw, vw, q_hbm, do_hbm, bias_hbm, att_hbm, qg_hbm, out,
         asm, inv, tab, wpad, q, do, bias, bias_t, wall, perm, wk, wv, qo, pp, r, tabs, stab, F, O, sb, sbo, rg,
         yr, yro, yso, acc, oc, zr, zo, of, ssem, rsem, lsem):
    y, z, x, c, dev = places()
    bf, f32 = jnp.bfloat16, jnp.float32
    scale = 1.0 / math.sqrt(HDIM)
    spans = r.shape[0]
    rows = spans * SPAN
    loads = [
        pltpu.make_async_copy(a, b, lsem.at[i])
        for i, (a, b) in enumerate(((bias_hbm, bias), (q_hbm, q), (do_hbm, do)))
    ]
    for cp in loads:
        cp.start()
    for j in range(2):
        F[j] = pool[j]
    mine = pl.ds(pl.multiple_of((2 * x + c) * 256, 256), 256)
    for k, w in enumerate((kw, vw)):
        wpad[...] = jnp.zeros_like(wpad)
        wpad[0:14] = w[:, mine].astype(f32)
        wall[0, 0, 0, 0, k] = wpad[...].astype(bf)
    reads = []
    down = lax.broadcasted_iota(jnp.int32, (8, 128), 0)
    along = lax.broadcasted_iota(jnp.int32, (8, 128), 1)
    wish = jnp.zeros((8, 128), jnp.int32)
    for i in range(spans):
        for j in range(2):
            pos = place[near[j, i]]
            owner, which = pos >> 1, pos & 1
            oy, oz = owner >> 3, owner & 7
            wish = jnp.where((down == oy) & (along == oz), which, wish)
            dy, dz = (y - oy) & 3, (z - oz) & 7
            far = jnp.where(dy == 1, 16, jnp.where(dy == 3, 24, 32)) + dz
            asm[2 * i + j] = jnp.where(dy == 0, 2 * dz + which, far)
            reads.append((dy * NZ + dz, which))
    tab[...] = wish
    barrier(dev, ["Y+", "Y-", "YO", "Z+", "Z-", "X+", "X-", "C"])
    L = Link(dev, ssem, rsem)

    def got(cps):
        for cp in cps:
            cp.wait_recv()

    tcp = [
        L.send(tab, tabs.at[k], to, "tab") for k, to in enumerate(("Y+", "Y-", "YO"))
    ]
    w1 = [
        L.send(wall.at[0, 0, 0, 0], wall.at[0, 0, 0, k], to, "w1")
        for k, to in ((1, "Y+"), (3, "Y-"), (2, "YO"))
    ]

    def own(k, j):
        a, b = k - 1, (NZ - k + 1) % NZ
        cps = []
        if k < 4 or j == 0:
            cps.append(L.send(F.at[2 * a + j], F.at[2 * k + j], "Z+", "block"))
        if k < 4 or j == 1:
            cps.append(L.send(F.at[2 * b + j], F.at[2 * (NZ - k) + j], "Z-", "block"))
        return cps

    def opp(k):
        a, b, m = k - 1, (NZ - k + 1) % NZ, NZ - k
        if k == 4:
            return [L.send(O.at[6], O.at[8], "Z+", "low"), L.send(O.at[11], O.at[9], "Z-", "low")]
        return [
            L.send(O.at[pl.ds(2 * a, 2)], O.at[pl.ds(2 * k, 2)], "Z+", "low"),
            L.send(O.at[pl.ds(2 * b, 2)], O.at[pl.ds(2 * m, 2)], "Z-", "low"),
        ]

    def weights(k):
        if k == 4:
            return [
                L.send(wall.at[0, 0, 5, pl.ds(0, 2)], wall.at[0, 0, 7, pl.ds(0, 2)], "Z+", "wz"),
                L.send(wall.at[0, 0, 6, pl.ds(2, 2)], wall.at[0, 0, 7, pl.ds(2, 2)], "Z-", "wz"),
            ]
        a, b = (0, 0) if k == 1 else (2 * k - 3, 2 * k - 2)
        return [
            L.send(wall.at[0, 0, a], wall.at[0, 0, 2 * k - 1], "Z+", "wz"),
            L.send(wall.at[0, 0, b], wall.at[0, 0, 2 * k], "Z-", "wz"),
        ]

    xs = {}
    to_core = [L.group() for _ in range(NX)]
    xf = L.group()

    def pieces(k):
        return pl.ds(0, 1) if k == 0 else pl.ds(7, 1) if k == 4 else pl.ds(2 * k - 1, 2)

    def core(dx, at):
        L.send(wall.at[dx, 0, at], wall.at[dx, 1, at], "C", "core", to_core[dx])

    def across(k):
        at = pieces(k)
        xs[k] = (
            L.send(wall.at[0, 0, at], wall.at[1, 0, at], "X+", "x"),
            L.send(wall.at[0, 0, at], wall.at[3, 0, at], "X-", "x"),
        )
        core(0, at)

    def across_on(k):
        got(xs[k])
        if k < 4:
            at = max(2 * k - 1, 0)
            L.send(wall.at[1, 0, at], wall.at[2, 0, at], "X+", "xf", xf)
        if k > 0:
            at = min(2 * k, 7)
            L.send(wall.at[3, 0, at], wall.at[2, 0, at], "X-", "xf", xf)
        core(1, pieces(k))
        core(3, pieces(k))

    direct, direct_top = L.group(), L.group()

    def ysend(d):
        zp = (z - d + NZ) % NZ
        sb[2 * d] = lax.select(stab[1, y, zp] > 0, F[2 * d + 1], F[2 * d])
        L.send(sb.at[2 * d], F.at[16 + d], "Y+", "block", direct)
        sb[2 * d + 1] = lax.select(stab[0, y, zp] > 0, F[2 * d + 1], F[2 * d])
        L.send(sb.at[2 * d + 1], F.at[24 + d], "Y-", "block", direct)
        sbo[d] = lax.select(stab[2, y, zp] > 0, F[2 * d + 1, 0:TOP], F[2 * d, 0:TOP])
        L.send(sbo.at[d], F.at[32 + d, pl.ds(0, TOP)], "YO", "top", direct_top)

    def project(dx, cc):
        if cc:
            L.landed(wall.at[dx, 1], to_core[dx])
        b = ((x - dx + NX) % NX) * 2 + (c + cc) % 2
        wide = pl.ds(pl.multiple_of(b * 256, 256), 256)
        pm = perm[...]
        for kv, w, src, base in ((0, wk, q, 0), (1, wv, do, HEADS * SPAN)):
            part = wall[dx, cc, :, :, kv].reshape(512, 256)
            wb = jnp.dot(pm, part, preferred_element_type=f32).astype(bf)
            w[:, wide] = wb
            rows_in = src[:, wide]
            for hh in range(2):
                t = nt(rows_in[:, hh * HDIM:(hh + 1) * HDIM], wb[:, hh * HDIM:(hh + 1) * HDIM])
                if kv == 0:
                    t = t * scale
                at = pl.ds(pl.multiple_of(base + b * 128 + hh * SPAN, SPAN), SPAN)
                qo[:, at] = t.astype(bf).reshape(spans, SPAN, E)

    o1 = [own(1, 0)]
    ex = L.send(F.at[pl.ds(0, 2), pl.ds(TOP, LOW)], O.at[pl.ds(0, 2)], "YO", "ex")
    got(w1)
    wz = weights(1)
    o1.append(own(1, 1))
    across(0)
    got(tcp)
    lc = [pltpu.make_async_copy(tabs.at[k], stab.at[k], lsem.at[3 + k]) for k in range(3)]
    for cp in lc:
        cp.start()
    for cp in lc:
        cp.wait()
    ysend(0)
    got(wz)
    wz = weights(2)
    got(o1[0])
    o2 = [own(2, 0)]
    got(o1[1])
    o2.append(own(2, 1))
    ysend(1)
    ysend(7)
    across(1)
    got(wz)
    wz = weights(3)
    got([ex])
    oz = opp(1)
    across_on(0)
    across(2)
    loads[0].wait()
    bias_t[...] = bias[...].T
    got(o2[0])
    o3 = [own(3, 0)]

    def find(k, _):
        read, which = jnp.int32(len(reads)), jnp.int32(0)
        for n, (owner, w) in enumerate(reads):
            read = jnp.where(owner == k, n, read)
            which = jnp.where(owner == k, w, which)
        inv[k] = read
        inv[32 + k] = which
        return 0

    lax.fori_loop(0, 32, find, 0)
    col = lax.broadcasted_iota(jnp.int32, (E, 512), 1)
    row = lax.broadcasted_iota(jnp.int32, (E, 512), 0)
    slot, dy, t = col >> 6, (col >> 4) & 3, col & 15
    dz = jnp.where((slot & 1) > 0, (slot + 1) >> 1, -((slot + 1) >> 1))
    source = (((y - dy) & 3) * NZ + ((z - dz) & 7)) * 14 + t
    perm[...] = jnp.where((source == row) & (t < 14), 1.0, 0.0).astype(bf)
    got(o2[1])
    ysend(2)
    ysend(6)
    got(wz)
    wz = weights(4)
    o3.append(own(3, 1))
    across_on(1)
    across(3)
    got(oz)
    oz = opp(2)
    across_on(2)
    got(wz)
    across(4)
    loads[1].wait()
    loads[2].wait()
    got(o3[0])
    got(o3[1])
    o4 = own(4, 0) + own(4, 1)
    ysend(3)
    ysend(5)
    across_on(3)
    project(0, 0)
    got(oz)
    oz = opp(3)
    across_on(4)
    project(0, 1)
    project(1, 0)
    got(o4)
    ysend(4)
    project(3, 0)
    L.landed(wall.at[2, 0], xf)
    core(2, pl.ds(0, NZ))
    got(oz)
    oz = opp(4)
    project(1, 1)
    project(3, 1)
    project(2, 0)
    project(2, 1)
    got(oz)
    L.landed(F.at[pl.ds(16, 16)], direct)
    L.landed(F.at[pl.ds(32, 8), pl.ds(0, TOP)], direct_top)
    for d in range(NZ):
        F[32 + d, TOP:448] = lax.select(inv[48 + d] > 0, O[2 * d + 1], O[2 * d])
    for i in range(spans):
        for j in range(2):
            r[i, j * NB:(j + 1) * NB] = F[asm[2 * i + j]].T
    for ref, kind in (
        (tabs, "tab"), (wall.at[0, 0, 0, pl.ds(0, 3)], "w1"), (wall.at[0, 0, pl.ds(0, 7)], "wz"),
        (wall.at[pl.ds(0, 2), 0], "x"), (wall.at[0, 0], "xf"), (wall.at[:, 0], "core"),
        (F.at[pl.ds(0, 30)], "block"), (O.at[pl.ds(0, 14)], "low"), (sbo, "top"),
        (O.at[pl.ds(0, 2)], "ex"),
    ):
        L.gone(ref, kind)

    half = HEADS * SPAN

    def stage1(i):
        return nt(r[i], qo[i, 0:half]) + bias_t[...], nt(r[i], qo[i, half:])

    def stage2(i, s, pg):
        e = jnp.exp(s - jnp.max(s, axis=0, keepdims=True))
        p = e * (1.0 / jnp.sum(e, axis=0, keepdims=True))
        low = p.astype(bf)
        delta = jnp.sum(low.astype(f32) * pg, axis=0, keepdims=True)
        ds = (p * (pg - delta)).astype(bf)
        pp[i, :, 0:half] = ds
        pp[i, :, half:] = low
        return ds, low

    def stage3(i, ds, low):
        g = jnp.dot(ds, qo[i, 0:half], preferred_element_type=f32)
        g = (g + jnp.dot(low, qo[i, half:], preferred_element_type=f32)).astype(bf)
        rg[2 * i] = g[0:NB].T
        rg[2 * i + 1] = g[NB:].T

    ahead, behind = stage1(0), None
    for i in range(spans):
        later = stage1(i + 1) if i + 1 < spans else None
        now = stage2(i, *ahead)
        if behind is not None:
            stage3(i - 1, *behind)
        ahead, behind = later, now
    stage3(spans - 1, *behind)
    rg[2 * spans] = jnp.zeros((448, 128), bf)

    back = {}

    def yslots(d):
        sb[2 * d] = rg[inv[8 + d]]
        group = L.group()
        L.send(sb.at[2 * d], yr.at[2 * d + 1], "Y-", "block", group)
        sb[2 * d + 1] = rg[inv[24 + d]]
        L.send(sb.at[2 * d + 1], yr.at[2 * d], "Y+", "block", group)
        yso[d] = rg[inv[16 + d], 0:TOP2]
        back[d] = group, L.send(yso.at[d], yro.at[d], "YO", "top")

    def back_home(d):
        group, top = back[d]
        L.landed(yr.at[pl.ds(2 * d, 2)], group)
        top.wait_recv()

    def dense(d):
        v = rg[inv[16 + d], TOP2:448]
        s = inv[48 + d]
        zero = jnp.zeros_like(v)
        oc[2 * d] = lax.select(s > 0, zero, v)
        oc[2 * d + 1] = lax.select(s > 0, v, zero)

    def pick(terms, j):
        t = None
        for v, s in terms:
            v = v.astype(f32)
            zero = jnp.zeros_like(v)
            v = lax.select(s > 0, v, zero) if j else lax.select(s > 0, zero, v)
            t = v if t is None else t + v
        return t

    def row_sum(d, j):
        zp = (z - d + NZ) % NZ
        s0, s1, s2 = tabs_at(0, zp), tabs_at(1, zp), tabs_at(2, zp)
        mine = rg[inv[d]]
        near = [(mine, inv[32 + d]), (yr[2 * d], s0), (yr[2 * d + 1], s1)]
        top = [(v[0:TOP2], s) for v, s in near] + [(yro[d], s2)]
        return pick(top, j), pick([(v[TOP2:448], s) for v, s in near], j)

    def tabs_at(k, zp):
        return stab[k, y, zp]

    def add_block(d, j, extra):
        top, low = row_sum(d, j)
        for ref in extra:
            top = top + ref[0:TOP2].astype(f32)
            low = low + ref[TOP2:448].astype(f32)
        return top, low

    group = 4 * SPAN
    outs = []

    def mix(g, base):
        for i in range(spans):
            t = tn(pp[i, :, base + g * group:base + (g + 1) * group], r[i])
            qo[i, base + g * group:base + (g + 1) * group] = t.astype(bf)

    def emit(g, base, w, dst, hbm, k):
        for h in range(4 * g, 4 * g + 4):
            v = qo[:, base + h * SPAN:base + (h + 1) * SPAN].reshape(rows, E)
            t = jnp.dot(v, w[:, h * HDIM:(h + 1) * HDIM], preferred_element_type=f32)
            if k == 1:
                t = t * scale
            dst[:, h * HDIM:(h + 1) * HDIM] = t.astype(bf)
        cols = pl.ds(4 * g * HDIM, 4 * HDIM)
        cp = pltpu.make_async_copy(dst.at[:, cols], hbm.at[:, cols], lsem.at[6 + 2 * g + k])
        cp.start()
        outs.append(cp)

    tasks = []
    for g in range(4):
        tasks.append(functools.partial(mix, g, half))
        tasks.append(functools.partial(emit, g, half, wv, q, att_hbm, 0))
        tasks.append(functools.partial(mix, g, 0))
        tasks.append(functools.partial(emit, g, 0, wk, do, qg_hbm, 1))

    def work(n):
        for _ in range(n):
            if tasks:
                tasks.pop(0)()

    def add_to(ref, i, n, src, k):
        for a in range(n):
            ref[i + a] = (ref[i + a].astype(f32) + src[k + a].astype(f32)).astype(bf)

    yslots(4)
    dense(4)
    oz = [L.send(oc.at[8], zo.at[0], "Z-", "low"), L.send(oc.at[9], zo.at[7], "Z+", "low")]
    yslots(3)
    yslots(5)
    dense(3)
    dense(5)
    yslots(2)
    yslots(6)
    yslots(1)
    yslots(7)
    yslots(0)
    for d in (2, 6, 1, 7, 0):
        dense(d)

    def own_back(e, prev):
        if e == 4:
            back_home(4)
            cps = []
            for j, to, at in ((0, "Z-", 0), (1, "Z+", 7)):
                top, low = row_sum(4, j)
                acc[8 + j, 0:TOP2] = top.astype(bf)
                acc[8 + j, TOP2:448] = low.astype(bf)
                cps.append(L.send(acc.at[8 + j], zr.at[at], to, "block"))
            return cps
        f = NZ - e
        back_home(e)
        back_home(f)
        at = 1 + 2 * (3 - e)
        cps = []
        for j in range(2):
            for d, base, to in ((e, 0, "Z-"), (f, 7, "Z+")):
                extra = []
                if e == 3:
                    if (j == 0) == (base == 0):
                        prev[base // 7].wait_recv()
                        extra = [zr.at[base]]
                else:
                    prev[2 * j + base // 7].wait_recv()
                    extra = [zr.at[base + at - 2 + j]]
                top, low = add_block(d, j, extra)
                acc[2 * d + j, 0:TOP2] = top.astype(bf)
                acc[2 * d + j, TOP2:448] = low.astype(bf)
                cps.append(L.send(acc.at[2 * d + j], zr.at[base + at + j], to, "block"))
        return cps

    def opp_back(e):
        got(oz)
        f = NZ - e
        if e == 3:
            add_to(oc, 6, 1, zo, 0)
            add_to(oc, 11, 1, zo, 7)
        elif e > 0:
            add_to(oc, 2 * e, 2, zo, 1 + 2 * (2 - e))
            add_to(oc, 2 * f, 2, zo, 8 + 2 * (2 - e))
        else:
            for j in range(2):
                t = oc[j].astype(f32) + zo[5 + j].astype(f32) + zo[12 + j].astype(f32)
                oc[j] = t.astype(bf)
            return [L.send(oc.at[pl.ds(0, 2)], of, "YO", "ex")]
        at = 1 + 2 * (3 - e)
        return [
            L.send(oc.at[pl.ds(2 * e, 2)], zo.at[pl.ds(at, 2)], "Z-", "low"),
            L.send(oc.at[pl.ds(2 * f, 2)], zo.at[pl.ds(7 + at, 2)], "Z+", "low"),
        ]

    work(1)
    oz = opp_back(3)
    work(1)
    oy = own_back(4, None)
    work(2)
    oz = opp_back(2)
    work(2)
    oy = own_back(3, oy)
    work(2)
    oz = opp_back(1)
    work(3)
    oy = own_back(2, oy)
    work(2)
    oz = opp_back(0)
    work(2)
    oy = own_back(1, oy)
    work(16)
    back_home(0)
    for j in range(2):
        got(oy[2 * j:2 * j + 2])
        if j == 0:
            got(oz)
        top, low = add_block(0, j, [zr.at[5 + j], zr.at[12 + j]])
        low = low + of[j].astype(f32)
        out[j, 0:TOP2] = top
        out[j, TOP2:448] = low
    for cp in outs:
        cp.wait()
    for ref, kind in (
        (F.at[pl.ds(0, 30)], "block"), (zo, "low"), (yso, "top"), (of, "ex"),
    ):
        L.gone(ref, kind)


def call(place, near, pool, kw, vw, q, do, bias):
    bf, f32 = jnp.bfloat16, jnp.float32
    rows = q.shape[0]
    spans = rows // SPAN
    sizes = (
        16, 64, ((8, 128), jnp.int32), ((16, 256), f32),
        ((rows, 2048), bf), ((rows, 2048), bf),
        ((HEADS * SPAN, 256), f32), ((256, HEADS * SPAN), f32),
        ((NX, 2, NZ, NY, 2, 16, 256), bf), ((E, 512), bf),
        ((E, 2048), bf), ((E, 2048), bf),
        ((spans, 2 * HEADS * SPAN, E), bf), ((spans, 256, 2 * HEADS * SPAN), bf),
        ((spans, 256, E), bf), ((3, 8, 128), jnp.int32), None,
        ((40, 448, 128), bf), ((16, LOW, 128), bf),
        ((16, 448, 128), bf), ((8, TOP, 128), bf), ((2 * spans + 1, 448, 128), bf),
        ((16, 448, 128), bf), ((8, TOP2, 128), bf), ((8, TOP2, 128), bf),
        ((16, 448, 128), bf), ((16, LOW2, 128), bf),
        ((14, 448, 128), bf), ((14, LOW2, 128), bf), ((2, LOW2, 128), bf),
    )
    scratch = [
        pltpu.SMEM((3, 8, 128), jnp.int32) if s is None
        else pltpu.SMEM((s,), jnp.int32) if isinstance(s, int)
        else pltpu.VMEM(*s) for s in sizes
    ]
    scratch += [
        pltpu.SemaphoreType.DMA((N_LEAVING,)), pltpu.SemaphoreType.DMA((N_LANDING,)),
        pltpu.SemaphoreType.DMA((14,)),
    ]
    hbm = pl.BlockSpec(memory_space=pl.ANY)
    return pl.pallas_call(
        body,
        out_shape=(
            jax.ShapeDtypeStruct(q.shape, bf),
            jax.ShapeDtypeStruct(q.shape, bf),
            jax.ShapeDtypeStruct((2, E, NB), f32),
        ),
        in_specs=[SM, SM, VM, VM, VM, hbm, hbm, hbm],
        out_specs=(hbm, hbm, VM),
        scratch_shapes=scratch,
        compiler_params=pltpu.CompilerParams(
            collective_id=0, has_side_effects=True, vmem_limit_bytes=VMEM_ASK
        ),
        name="retro",
    )(place, near, pool, kw, vw, q, do, bias)


def hand_over(*refs):
    n = 4
    src, dst, mid, sem = refs[0:3], refs[3:6], refs[6:9], refs[9]
    ins, outs = [], []
    for k in range(n):
        for a, m, b in zip(src[0:2], mid[0:2], dst[0:2]):
            part = pl.ds(k * (a.shape[0] // n), a.shape[0] // n)
            i = len(ins)
            ins.append(pltpu.make_async_copy(a.at[part], m.at[part], sem.at[2 * i]))
            outs.append(pltpu.make_async_copy(m.at[part], b.at[part], sem.at[2 * i + 1]))
    ins.append(pltpu.make_async_copy(src[2], mid[2], sem.at[4 * n]))
    outs.append(pltpu.make_async_copy(mid[2], dst[2], sem.at[4 * n + 1]))
    for cp in ins:
        cp.start()
    for a, b in zip(ins, outs):
        a.wait()
        b.start()
    for cp in outs:
        cp.wait()


def hand_over_call(*arrays):
    hbm = pl.BlockSpec(memory_space=pl.ANY)
    return pl.pallas_call(
        hand_over,
        out_shape=tuple(jax.ShapeDtypeStruct(a.shape, a.dtype) for a in arrays),
        in_specs=[hbm] * 3,
        out_specs=(hbm,) * 3,
        scratch_shapes=[pltpu.VMEM(a.shape, a.dtype) for a in arrays]
        + [pltpu.SemaphoreType.DMA((18,))],
        compiler_params=pltpu.CompilerParams(vmem_limit_bytes=VMEM_ASK),
        name="handover",
    )(*arrays)


def on_device(queries, cotangent, pool, key_weight, value_weight, score_bias, neighbours, place):
    bias = score_bias.reshape(HEADS * SPAN, 2 * NB)
    att, qg, pg = hand_over_call(*call(
        place, neighbours.T, jnp.transpose(pool, (0, 2, 1)), key_weight, value_weight,
        queries, cotangent, bias,
    ))
    return att, qg, jnp.transpose(pg, (0, 2, 1))


def solution(mesh):
    both = ("batch", "seq")
    in_specs = (
        P(both, None), P(both, None), P(both, None, None), P("seq", None), P("seq", None),
        P(), P(both, None), P("batch"),
    )
    out_specs = (P(both, None), P(both, None), P(both, None, None))
    return jax.shard_map(
        on_device, mesh=mesh, in_specs=in_specs, out_specs=out_specs, check_vma=False
    )
```

time: 106 us -> 95.3 us (0.90)
  local copies, waits for them, and re-layouts: 8.92 us -> 0 us
  other arithmetic: 2.26 us -> 0 us
    unnamed x13 -> x0, local copies, waits for them, and re-layouts: 4.87 us -> none
    pallas_call x1, Pallas kernels: 94.3 us -> 90.9 us  [call(): pl.pallas_call(body, out_shape=(jax.ShapeDtypeStruct(q.shape, bf), jax.Sh...]
    pallas_call x0 -> x1, Pallas kernels: none -> 3.06 us  [hand_over_call(): pl.pallas_call(hand_over, out_shape=tuple((jax.ShapeDtypeStruct(a.shape,...]
    pallas_call x1 -> x0, local copies, waits for them, and re-layouts: 2.01 us -> none  [call(): pl.pallas_call(body, out_shape=(jax.ShapeDtypeStruct(q.shape, bf), jax.Sh...]
where the time goes in v3:
time: 95.3 us; the launch traced here: 94.8 us
  Pallas kernels  94 us (99%)
    pallas_call x1, Pallas kernels, call(): pl.pallas_call(body, out_shape=(jax.ShapeDtypeStruct(q.shape, bf), jax.Sh...  90.9 us
    pallas_call x1, Pallas kernels, hand_over_call(): pl.pallas_call(hand_over, out_shape=tuple((jax.ShapeDtypeStruct(a.shape,...  3.06 us

profile of v3, /device:TPU:4, one launch (start us, length us, event | category | flops | bytes accessed | tf_op | source)
XLA Modules:
  0.0 94.8 jit_solution(11753135381938388919)
XLA Ops:
  0.6 90.9 %retro.1 = (bf16[384,2048]{1,0:T(8,128)(2,1)}, bf16[384,2048]{1,0:T(8,128)(2,1)}, f32[2,448,128]{2,1,0:T(8,128)}) custom-call(s32[64]{0:T(128)} %place.1, s32[2,6]{1,0:T(2,128)} %bitcast.6, bf16[2,448,128]{2,1,0:T(8,128)(2,1)} %bitcast.5, bf16[14,2048]{1,0:T(8,128)(2,1)} %kw.1, bf16[14,2048]{1,0:T(8,128)(2,1)} %vw.1, bf16[384,2048]{1,0:T(8,128)(2,1)} %q_hbm.1, ...), custom_call_target="tpu_custom_call" | custom-call | tf_op jit(solution)/shard_map/retro/pallas_call | solution.py:580
  91.5 3.1 %handover.1 = (bf16[384,2048]{1,0:T(8,128)(2,1)}, bf16[384,2048]{1,0:T(8,128)(2,1)}, f32[2,448,128]{2,1,0:T(8,128)}) custom-call(bf16[384,2048]{1,0:T(8,128)(2,1)} %get-tuple-element.9.refs_0_, bf16[384,2048]{1,0:T(8,128)(2,1)} %get-tuple-element.10.refs_1_, f32[2,448,128]{2,1,0:T(8,128)} %get-tuple-element.11.refs_2_), custom_call_target="tpu_custom_call" | custom-call | tf_op jit(solution)/shard_map/handover/pallas_call | solution.py:620

commit v4 on v3

--- a/solution.py
+++ b/solution.py
@@ -16,9 +16,9 @@
 NY = 4
 NZ = 8
 NX = 4
-LOW = 208
+LOW = 176
 TOP = 448 - LOW
-LOW2 = 272
+LOW2 = 256
 TOP2 = 448 - LOW2
 MIB = 1024 * 1024
 VMEM_ASK = 63 * MIB
@@ -347,40 +347,46 @@
         pp[i, :, half:] = low
         return ds, low
 
-    def stage3(i, ds, low):
-        g = jnp.dot(ds, qo[i, 0:half], preferred_element_type=f32)
-        g = (g + jnp.dot(low, qo[i, half:], preferred_element_type=f32)).astype(bf)
-        rg[2 * i] = g[0:NB].T
-        rg[2 * i + 1] = g[NB:].T
+    def stage3(i, ds, low, part):
+        g = jnp.dot(ds, qo[i, 0:half, part], preferred_element_type=f32)
+        g = (g + jnp.dot(low, qo[i, half:, part], preferred_element_type=f32)).astype(bf)
+        rg[2 * i, part] = g[0:NB].T
+        rg[2 * i + 1, part] = g[NB:].T
+
+    first, second = slice(0, LOW2), slice(LOW2, 448)
 
     ahead, behind = stage1(0), None
     for i in range(spans):
         later = stage1(i + 1) if i + 1 < spans else None
         now = stage2(i, *ahead)
         if behind is not None:
-            stage3(i - 1, *behind)
+            stage3(i - 1, *behind, first)
         ahead, behind = later, now
-    stage3(spans - 1, *behind)
+    stage3(spans - 1, *behind, first)
     rg[2 * spans] = jnp.zeros((448, 128), bf)
 
     back = {}
 
-    def yslots(d):
-        sb[2 * d] = rg[inv[8 + d]]
-        group = L.group()
-        L.send(sb.at[2 * d], yr.at[2 * d + 1], "Y-", "block", group)
-        sb[2 * d + 1] = rg[inv[24 + d]]
-        L.send(sb.at[2 * d + 1], yr.at[2 * d], "Y+", "block", group)
-        yso[d] = rg[inv[16 + d], 0:TOP2]
-        back[d] = group, L.send(yso.at[d], yro.at[d], "YO", "top")
+    def yslots(d, part):
+        if d not in back:
+            back[d] = L.group(), L.group()
+        group, top = back[d]
+        rows_at = pl.ds(part.start, part.stop - part.start)
+        sb[2 * d, part] = rg[inv[8 + d], part]
+        L.send(sb.at[2 * d, rows_at], yr.at[2 * d + 1, rows_at], "Y-", "block", group)
+        sb[2 * d + 1, part] = rg[inv[24 + d], part]
+        L.send(sb.at[2 * d + 1, rows_at], yr.at[2 * d, rows_at], "Y+", "block", group)
+        if part.stop == 448:
+            yso[d] = rg[inv[16 + d], second]
+            L.send(yso.at[d], yro.at[d], "YO", "top", top)
 
     def back_home(d):
         group, top = back[d]
         L.landed(yr.at[pl.ds(2 * d, 2)], group)
-        top.wait_recv()
+        L.landed(yro.at[d], top)
 
     def dense(d):
-        v = rg[inv[16 + d], TOP2:448]
+        v = rg[inv[16 + d], first]
         s = inv[48 + d]
         zero = jnp.zeros_like(v)
         oc[2 * d] = lax.select(s > 0, zero, v)
@@ -400,8 +406,8 @@
         s0, s1, s2 = tabs_at(0, zp), tabs_at(1, zp), tabs_at(2, zp)
         mine = rg[inv[d]]
         near = [(mine, inv[32 + d]), (yr[2 * d], s0), (yr[2 * d + 1], s1)]
-        top = [(v[0:TOP2], s) for v, s in near] + [(yro[d], s2)]
-        return pick(top, j), pick([(v[TOP2:448], s) for v, s in near], j)
+        top = [(v[second], s) for v, s in near] + [(yro[d], s2)]
+        return pick(top, j), pick([(v[first], s) for v, s in near], j)
 
     def tabs_at(k, zp):
         return stab[k, y, zp]
@@ -409,8 +415,8 @@
     def add_block(d, j, extra):
         top, low = row_sum(d, j)
         for ref in extra:
-            top = top + ref[0:TOP2].astype(f32)
-            low = low + ref[TOP2:448].astype(f32)
+            top = top + ref[second].astype(f32)
+            low = low + ref[first].astype(f32)
         return top, low
 
     group = 4 * SPAN
@@ -449,18 +455,19 @@
         for a in range(n):
             ref[i + a] = (ref[i + a].astype(f32) + src[k + a].astype(f32)).astype(bf)
 
-    yslots(4)
+    yslots(4, first)
     dense(4)
     oz = [L.send(oc.at[8], zo.at[0], "Z-", "low"), L.send(oc.at[9], zo.at[7], "Z+", "low")]
-    yslots(3)
-    yslots(5)
+    yslots(3, first)
+    yslots(5, first)
+    for i in range(spans):
+        stage3(i, pp[i, :, 0:half], pp[i, :, half:], second)
+    for d in (4, 3, 5):
+        yslots(d, second)
     dense(3)
     dense(5)
-    yslots(2)
-    yslots(6)
-    yslots(1)
-    yslots(7)
-    yslots(0)
+    for d in (2, 6, 1, 7, 0):
+        yslots(d, slice(0, 448))
     for d in (2, 6, 1, 7, 0):
         dense(d)
 
@@ -470,8 +477,8 @@
             cps = []
             for j, to, at in ((0, "Z-", 0), (1, "Z+", 7)):
                 top, low = row_sum(4, j)
-                acc[8 + j, 0:TOP2] = top.astype(bf)
-                acc[8 + j, TOP2:448] = low.astype(bf)
+                acc[8 + j, second] = top.astype(bf)
+                acc[8 + j, first] = low.astype(bf)
                 cps.append(L.send(acc.at[8 + j], zr.at[at], to, "block"))
             return cps
         f = NZ - e
@@ -490,8 +497,8 @@
                     prev[2 * j + base // 7].wait_recv()
                     extra = [zr.at[base + at - 2 + j]]
                 top, low = add_block(d, j, extra)
-                acc[2 * d + j, 0:TOP2] = top.astype(bf)
-                acc[2 * d + j, TOP2:448] = low.astype(bf)
+                acc[2 * d + j, second] = top.astype(bf)
+                acc[2 * d + j, first] = low.astype(bf)
                 cps.append(L.send(acc.at[2 * d + j], zr.at[base + at + j], to, "block"))
         return cps
 
@@ -539,8 +546,8 @@
             got(oz)
         top, low = add_block(0, j, [zr.at[5 + j], zr.at[12 + j]])
         low = low + of[j].astype(f32)
-        out[j, 0:TOP2] = top
-        out[j, TOP2:448] = low
+        out[j, second] = top
+        out[j, first] = low
     for cp in outs:
         cp.wait()
     for ref, kind in (

time: 95.3 us -> 92.8 us (0.974)
  Pallas kernels: 94 us -> 91.8 us
    pallas_call x1, Pallas kernels: 90.9 us -> 88.8 us  [call(): pl.pallas_call(body, out_shape=(jax.ShapeDtypeStruct(q.shape, bf), jax.Sh...]
where the time goes in v4:
time: 92.8 us; the launch traced here: 92.6 us
  Pallas kernels  91.8 us (99%)
    pallas_call x1, Pallas kernels, call(): pl.pallas_call(body, out_shape=(jax.ShapeDtypeStruct(q.shape, bf), jax.Sh...  88.8 us
    pallas_call x1, Pallas kernels, hand_over_call(): pl.pallas_call(hand_over, out_shape=tuple((jax.ShapeDtypeStruct(a.shape,...  3.06 us

profile of v4, /device:TPU:4, one launch (start us, length us, event | category | flops | bytes accessed | tf_op | source)
XLA Modules:
  0.0 92.6 jit_solution(9703762275028623057)
XLA Ops:
  0.6 88.8 %retro.1 = (bf16[384,2048]{1,0:T(8,128)(2,1)}, bf16[384,2048]{1,0:T(8,128)(2,1)}, f32[2,448,128]{2,1,0:T(8,128)}) custom-call(s32[64]{0:T(128)} %place.1, s32[2,6]{1,0:T(2,128)} %bitcast.6, bf16[2,448,128]{2,1,0:T(8,128)(2,1)} %bitcast.5, bf16[14,2048]{1,0:T(8,128)(2,1)} %kw.1, bf16[14,2048]{1,0:T(8,128)(2,1)} %vw.1, bf16[384,2048]{1,0:T(8,128)(2,1)} %q_hbm.1, ...), custom_call_target="tpu_custom_call" | custom-call | tf_op jit(solution)/shard_map/retro/pallas_call | solution.py:587
  89.4 3.1 %handover.1 = (bf16[384,2048]{1,0:T(8,128)(2,1)}, bf16[384,2048]{1,0:T(8,128)(2,1)}, f32[2,448,128]{2,1,0:T(8,128)}) custom-call(bf16[384,2048]{1,0:T(8,128)(2,1)} %get-tuple-element.9.refs_0_, bf16[384,2048]{1,0:T(8,128)(2,1)} %get-tuple-element.10.refs_1_, f32[2,448,128]{2,1,0:T(8,128)} %get-tuple-element.11.refs_2_), custom_call_target="tpu_custom_call" | custom-call | tf_op jit(solution)/shard_map/handover/pallas_call | solution.py:627

commit v5 on v4

--- a/solution.py
+++ b/solution.py
@@ -75,7 +75,7 @@
     sem = pltpu.get_barrier_semaphore()
     for n in names:
         pl.semaphore_signal(sem, inc=1, device_id=dev[n], device_id_type=MESH)
-    pl.semaphore_wait(sem, len(names))
+    return sem, len(names)
 
 
 def nt(a, b):
@@ -86,18 +86,19 @@
     return lax.dot_general(a, b, (((0,), (0,)), ((), ())), preferred_element_type=jnp.float32)
 
 
-N_LANDING = 93
+N_LANDING = 89
 N_LEAVING = 10
 
 
 def body(place, near, pool, kw, vw, q_hbm, do_hbm, bias_hbm, att_hbm, qg_hbm, out,
          asm, inv, tab, wpad, q, do, bias, bias_t, wall, perm, wk, wv, qo, pp, r, tabs, stab, F, O, sb, sbo, rg,
-         yr, yro, yso, acc, oc, zr, zo, of, ssem, rsem, lsem):
+         yr, yro, yso, acc, oc, zr, zo, of, res, ssem, rsem, lsem):
     y, z, x, c, dev = places()
     bf, f32 = jnp.bfloat16, jnp.float32
     scale = 1.0 / math.sqrt(HDIM)
     spans = r.shape[0]
     rows = spans * SPAN
+    met = barrier(dev, ["Y+", "Y-", "YO", "Z+", "Z-", "X+", "X-", "C"])
     loads = [
         pltpu.make_async_copy(a, b, lsem.at[i])
         for i, (a, b) in enumerate(((bias_hbm, bias), (q_hbm, q), (do_hbm, do)))
@@ -126,18 +127,19 @@
             asm[2 * i + j] = jnp.where(dy == 0, 2 * dz + which, far)
             reads.append((dy * NZ + dz, which))
     tab[...] = wish
-    barrier(dev, ["Y+", "Y-", "YO", "Z+", "Z-", "X+", "X-", "C"])
+    pl.semaphore_wait(*met)
     L = Link(dev, ssem, rsem)
 
     def got(cps):
         for cp in cps:
             cp.wait_recv()
 
+    tg, wg = L.group(), L.group()
     tcp = [
-        L.send(tab, tabs.at[k], to, "tab") for k, to in enumerate(("Y+", "Y-", "YO"))
+        L.send(tab, tabs.at[k], to, "tab", tg) for k, to in enumerate(("Y+", "Y-", "YO"))
     ]
     w1 = [
-        L.send(wall.at[0, 0, 0, 0], wall.at[0, 0, 0, k], to, "w1")
+        L.send(wall.at[0, 0, 0, 0], wall.at[0, 0, 0, k], to, "w1", wg)
         for k, to in ((1, "Y+"), (3, "Y-"), (2, "YO"))
     ]
 
@@ -231,11 +233,11 @@
 
     o1 = [own(1, 0)]
     ex = L.send(F.at[pl.ds(0, 2), pl.ds(TOP, LOW)], O.at[pl.ds(0, 2)], "YO", "ex")
-    got(w1)
+    L.landed(wall.at[0, 0, 0, pl.ds(1, 3)], wg)
     wz = weights(1)
     o1.append(own(1, 1))
     across(0)
-    got(tcp)
+    L.landed(tabs, tg)
     lc = [pltpu.make_async_copy(tabs.at[k], stab.at[k], lsem.at[3 + k]) for k in range(3)]
     for cp in lc:
         cp.start()
@@ -546,8 +548,11 @@
             got(oz)
         top, low = add_block(0, j, [zr.at[5 + j], zr.at[12 + j]])
         low = low + of[j].astype(f32)
-        out[j, second] = top
-        out[j, first] = low
+        res[j, second] = top
+        res[j, first] = low
+        cp = pltpu.make_async_copy(res.at[j], out.at[j], lsem.at[14 + j])
+        cp.start()
+        outs.append(cp)
     for cp in outs:
         cp.wait()
     for ref, kind in (
@@ -573,6 +578,7 @@
         ((16, 448, 128), bf), ((8, TOP2, 128), bf), ((8, TOP2, 128), bf),
         ((16, 448, 128), bf), ((16, LOW2, 128), bf),
         ((14, 448, 128), bf), ((14, LOW2, 128), bf), ((2, LOW2, 128), bf),
+        ((2, E, NB), f32),
     )
     scratch = [
         pltpu.SMEM((3, 8, 128), jnp.int32) if s is None
@@ -581,7 +587,7 @@
     ]
     scratch += [
         pltpu.SemaphoreType.DMA((N_LEAVING,)), pltpu.SemaphoreType.DMA((N_LANDING,)),
-        pltpu.SemaphoreType.DMA((14,)),
+        pltpu.SemaphoreType.DMA((16,)),
     ]
     hbm = pl.BlockSpec(memory_space=pl.ANY)
     return pl.pallas_call(
@@ -592,7 +598,7 @@
             jax.ShapeDtypeStruct((2, E, NB), f32),
         ),
         in_specs=[SM, SM, VM, VM, VM, hbm, hbm, hbm],
-        out_specs=(hbm, hbm, VM),
+        out_specs=(hbm, hbm, hbm),
         scratch_shapes=scratch,
         compiler_params=pltpu.CompilerParams(
             collective_id=0, has_side_effects=True, vmem_limit_bytes=VMEM_ASK

time: 92.8 us -> 92.6 us (level)
  no operation moved by 1% of the time
where the time goes in v5:
time: 92.6 us; the launch traced here: 92.5 us
  Pallas kernels  91.7 us (99%)
    pallas_call x1, Pallas kernels, call(): pl.pallas_call(body, out_shape=(jax.ShapeDtypeStruct(q.shape, bf), jax.Sh...  88.6 us
    pallas_call x1, Pallas kernels, hand_over_call(): pl.pallas_call(hand_over, out_shape=tuple((jax.ShapeDtypeStruct(a.shape,...  3.06 us

profile of v5, /device:TPU:4, one launch (start us, length us, event | category | flops | bytes accessed | tf_op | source)
XLA Modules:
  0.0 92.5 jit_solution(282810596080038899)
XLA Ops:
  0.6 88.6 %retro.1 = (bf16[384,2048]{1,0:T(8,128)(2,1)}, bf16[384,2048]{1,0:T(8,128)(2,1)}, f32[2,448,128]{2,1,0:T(8,128)}) custom-call(s32[64]{0:T(128)} %place.1, s32[2,6]{1,0:T(2,128)} %bitcast.6, bf16[2,448,128]{2,1,0:T(8,128)(2,1)} %bitcast.5, bf16[14,2048]{1,0:T(8,128)(2,1)} %kw.1, bf16[14,2048]{1,0:T(8,128)(2,1)} %vw.1, bf16[384,2048]{1,0:T(8,128)(2,1)} %q_hbm.1, ...), custom_call_target="tpu_custom_call" | custom-call | tf_op jit(solution)/shard_map/retro/pallas_call | solution.py:593
  89.3 3.1 %handover.1 = (bf16[384,2048]{1,0:T(8,128)(2,1)}, bf16[384,2048]{1,0:T(8,128)(2,1)}, f32[2,448,128]{2,1,0:T(8,128)}) custom-call(bf16[384,2048]{1,0:T(8,128)(2,1)} %get-tuple-element.9.refs_0_, bf16[384,2048]{1,0:T(8,128)(2,1)} %get-tuple-element.10.refs_1_, f32[2,448,128]{2,1,0:T(8,128)} %get-tuple-element.11.refs_2_), custom_call_target="tpu_custom_call" | custom-call | tf_op jit(solution)/shard_map/handover/pallas_call | solution.py:633
